TPU v7x, 32 devices: a whole 2x2x4 slice. The times are simulated.
32 devices in a mesh: parts: 2 (over x), height: 16 (over z, y, core).
Axes of the slice: x: 2, y: 2, z: 4, core: 2. Of those that a mesh axis runs over, the one named last changes fastest.
Arguments:
- snapshots: float32 [65536, 256], P(('parts', 'height')), parts along dimension 0
- fluid_mask: int32 [65536], P(('parts', 'height')), parts along dimension 0, may hold values from 0 to 1, as said below
Outputs:
- modes: float32 [32768, 256], P(('parts', 'height')), parts along dimension 0
- factor: float32 [512, 256], P('parts'), parts along dimension 0
There are 2 independent parts, one for each index of `parts`. A program takes and returns all parts, laid end to end along the dimension named above; each array names one. Nothing has to cross between parts.
Inputs may be any that keep to these rules, and one draw needn't show every extreme that they name: `fluid_mask`: each tile of 2048 cells holds 512 to 1536 fluid cells, some tile exactly 1536; all tiles together hold exactly 16384.
All inputs are finite; a program needn't handle non-finite values.
Results may differ from a plain program's by a relative error of at most 0.0003.
Values sent between devices are 32-bit elements; how exact they have to be, the bound alone decides.
No kernel may reach another device: no remote copies, remote signals or barrier semaphores. Data moves between devices by JAX's collectives and lax.ppermute only.
A program may use at most 64 MiB of HBM per device.

v0:
```python
import jax
import jax.numpy as jnp
from jax import lax
from jax.sharding import PartitionSpec as P

BLK = 1024
MAXC = 1536


highest_precision = lax.Precision.HIGHEST


def gram_matrix(row_block, row_total):
    return (
        lax.dot_general(
            row_block,
            row_block,
            (((0,), (0,)), ((), ())),
            precision=highest_precision,
            preferred_element_type=jnp.float32,
        )
        / row_total
    )


def upper_factor(gram_value):
    order_size = gram_value.shape[0]
    positions = jnp.arange(order_size, dtype=jnp.int32)

    def column_step(column, lower):
        column = column.astype(jnp.int32)
        row_of = lax.dynamic_slice_in_dim(lower, column, 1, 0)[0]
        target = lax.dynamic_slice_in_dim(gram_value, column, 1, 1)[:, 0]
        residue = target - jnp.dot(lower, row_of, precision=highest_precision)
        pivot = jnp.sqrt(jnp.sum(jnp.where(positions == column, residue, 0.0)))
        entries = jnp.where(positions >= column, residue / pivot, 0.0)
        return lax.dynamic_update_slice_in_dim(lower, entries[:, None], column, 1)

    lower = lax.fori_loop(0, order_size, column_step, jnp.zeros_like(gram_value))
    return lower.T


def inverse_upper(factor):
    order_size = factor.shape[0]
    positions = jnp.arange(order_size, dtype=jnp.int32)

    def row_step(offset, solved):
        row = (order_size - 1 - offset).astype(jnp.int32)
        factor_row = lax.dynamic_slice_in_dim(factor, row, 1, 0)[0]
        pivot = jnp.sum(jnp.where(positions == row, factor_row, 0.0))
        unit = jnp.where(positions == row, 1.0, 0.0).astype(factor.dtype)
        entries = (unit - jnp.dot(factor_row, solved, precision=highest_precision)) / pivot
        return lax.dynamic_update_slice_in_dim(solved, entries[None, :], row, 0)

    return lax.fori_loop(0, order_size, row_step, jnp.zeros_like(factor))


def product(left, right):
    return jnp.dot(left, right, precision=highest_precision, preferred_element_type=jnp.float32)


def combined_factor(local_gram):
    return upper_factor(lax.psum(local_gram, "height"))


def two_pass(row_block, row_total):
    first_factor = combined_factor(gram_matrix(row_block, row_total))
    first_basis = product(row_block, inverse_upper(first_factor))
    second_factor = combined_factor(gram_matrix(first_basis, row_total))
    modes = product(first_basis, inverse_upper(second_factor))
    return (modes, product(second_factor, first_factor))


def relay(source, send_index, live_slots, pick_rows):
    outgoing = jnp.take(source, send_index, axis=0) * live_slots[:, None].astype(source.dtype)
    received = lax.all_to_all(outgoing, "height", split_axis=0, concat_axis=0, tiled=True)
    return jnp.take(received, pick_rows, axis=0)


def local(snapshots, fluid_mask):
    tile_count = lax.axis_size("height")
    own_place = lax.axis_index("height")
    cell_count = snapshots.shape[0]
    most_rows = MAXC
    slot_count = (most_rows + tile_count - 1) // tile_count
    row_total = float(tile_count * BLK)
    own_count = jnp.sum(fluid_mask)
    counts = lax.all_gather(own_count.reshape(1), "height", axis=0, tiled=True)
    run_ends = jnp.cumsum(counts)
    own_start = jnp.sum(jnp.where(jnp.arange(tile_count, dtype=jnp.int32) < own_place, counts, 0))
    fluid_rank = jnp.cumsum(fluid_mask) - 1
    cell_of = (
        jnp.zeros((most_rows,), jnp.int32)
        .at[jnp.where(fluid_mask > 0, fluid_rank, most_rows)]
        .set(jnp.arange(cell_count, dtype=jnp.int32), mode="drop")
    )
    target = jnp.arange(tile_count, dtype=jnp.int32)[:, None]
    slot_step = jnp.arange(slot_count, dtype=jnp.int32)[None, :]
    first_row = (own_start - target + tile_count - 1) // tile_count
    fluid_index = target + tile_count * (first_row + slot_step) - own_start
    live_slots = (fluid_index < own_count).reshape(-1)
    send_index = jnp.clip(fluid_index, 0, most_rows - 1).reshape(-1)
    out_row = jnp.arange(BLK, dtype=jnp.int32)
    global_index = out_row * tile_count + own_place
    before = run_ends[None, :] <= global_index[:, None]
    source_tile = jnp.sum(before.astype(jnp.int32), axis=1)
    source_start = jnp.sum(jnp.where(before, counts[None, :], 0), axis=1)
    source_first = (source_start - own_place + tile_count - 1) // tile_count
    pick_rows = source_tile * slot_count + out_row - source_first
    balanced = relay(snapshots, jnp.take(cell_of, send_index), live_slots, pick_rows)
    modes, factor = two_pass(balanced, row_total)
    return (modes, factor)


def solution(mesh):
    return jax.shard_map(
        local,
        mesh=mesh,
        in_specs=(P(("parts", "height"), None), P(("parts", "height"))),
        out_specs=(P(("parts", "height"), None), P("parts", None)),
        check_vma=False,
    )
```

profile of v0, /device:TPU:13, one launch (start us, length us, event | category | flops | bytes accessed | tf_op | source)
XLA Modules:
  0.0 2379.4 jit_solution(13475010520676423007)
XLA Ops:
  7.2 1.1 reduce-window.20
  8.5 1.4 fusion.54
  9.9 1.2 dynamic-slice
  11.2 1.4 dynamic-update-slice
  12.6 7.9 all-reduce
  22.6 8.0 scatter_custom_fusion
  30.7 8.4 gather_fusion
  39.2 1.4 compare_and_fusion
  40.6 4.7 gather_fusion.1
  45.3 2.6 select_multiply_fusion
  47.9 9.3 all-to-all-start
  57.6 35.8 %all-to-all-done = f32[16,96,256]{2,1,0:T(8,128)} async-done(((f32[16,96,256]{2,1,0:T(8,128)}), f32[16,96,256]{2,1,0:T(8,128)}, u32[]{:S(2)}, u32[]{:S(2)}) %all-to-all-start) | async-done | bytes 1572896 | tf_op jit(solution)/shard_map/all_to_all | solution.py:76
  93.4 4.9 gather_fusion.2
  98.3 2.8 convolution_multiply_fusion.1
  101.4 87.4 %all-reduce.4.cloned.1.call-done = f32[256,256]{1,0:T(8,128)} async-done(((f32[256,256]{1,0:T(8,128)}), f32[256,256]{1,0:T(8,128)}) %all-reduce.4.cloned.1.call-update) | async-done | bytes 262160 | tf_op jit(solution)/shard_map/psum | solution.py:63
  188.8 1.1 copy.22
  189.9 622.4 %while.64 = (s32[]{:T(128)}, f32[256,256]{1,0:T(8,128)S(1)}, f32[256,256]{0,1:T(8,128)S(1)}, s32[]{:T(128)}, s32[]{:T(128)}) while((s32[]{:T(128)}, f32[256,256]{1,0:T(8,128)S(1)}, f32[256,256]{0,1:T(8,128)S(1)}, s32[]{:T(128)}, s32[]{:T(128)}) %tuple.159), condition=%wide.region_11.12_spmd.clone.clone, body=%wide.region_9.11_spmd.clone.clone.sunk | while | flops 788225 | bytes 275553 | solution.py:39
  812.4 402.7 %while.62 = (s32[]{:T(128)}, f32[256,256]{1,0:T(8,128)S(1)}, f32[256,256]{1,0:T(8,128)S(1)}, s32[]{:T(128)}, s32[]{:T(128)}, /*index=5*/s32[]{:T(128)}, s32[]{:T(128)}) while((s32[]{:T(128)}, f32[256,256]{1,0:T(8,128)S(1)}, f32[256,256]{1,0:T(8,128)S(1)}, s32[]{:T(128)}, s32[]{:T(128)}, /*index=5*/s32[]{:T(128)}, ...), condition=%wide.region_14.15_spmd.clone, body=%wide.region_12.14_spmd.clone.sunk | while | flops 788229 | bytes 271507 | solution.py:55
  1215.2 2.2 fusion.32
  1217.4 1.0 copy-done.1
  1218.4 2.5 convolution_multiply_fusion
  1221.0 89.5 %all-reduce.6.cloned.1.call-done = f32[256,256]{1,0:T(8,128)} async-done(((f32[256,256]{1,0:T(8,128)}), f32[256,256]{1,0:T(8,128)}) %all-reduce.6.cloned.1.call-update) | async-done | bytes 262160 | tf_op jit(solution)/shard_map/psum | solution.py:63
  1310.5 1.1 copy.24
  1311.6 622.4 %while.65 = (s32[]{:T(128)}, f32[256,256]{1,0:T(8,128)S(1)}, f32[256,256]{0,1:T(8,128)S(1)}, s32[]{:T(128)}, s32[]{:T(128)}) while((s32[]{:T(128)}, f32[256,256]{1,0:T(8,128)S(1)}, f32[256,256]{0,1:T(8,128)S(1)}, s32[]{:T(128)}, s32[]{:T(128)}) %tuple.165), condition=%wide.region_18.19_spmd.clone.clone, body=%wide.region_16.18_spmd.clone.clone.sunk | while | flops 788225 | bytes 275553 | solution.py:39
  1933.9 1.3 fusion.56
  1935.4 434.0 %while.63 = (s32[]{:T(128)}, f32[256,256]{1,0:T(8,128)S(1)}, f32[256,256]{1,0:T(8,128)S(1)}, s32[]{:T(128)}, s32[]{:T(128)}, /*index=5*/s32[]{:T(128)}, s32[]{:T(128)}) while((s32[]{:T(128)}, f32[256,256]{1,0:T(8,128)S(1)}, f32[256,256]{1,0:T(8,128)S(1)}, s32[]{:T(128)}, s32[]{:T(128)}, /*index=5*/s32[]{:T(128)}, ...), condition=%wide.region_21.22_spmd.clone, body=%wide.region_19.21_spmd.clone.sunk | while | flops 788229 | bytes 271507 | solution.py:55
  1936.3 0.7 fusion.95
  1944.8 0.7 fusion.95
  1946.5 0.7 fusion.95
  1954.9 0.7 fusion.95
  1956.6 0.7 fusion.95
  1965.1 0.7 fusion.95
  1966.8 0.7 fusion.95
  1968.5 0.7 fusion.95
  1977.0 0.7 fusion.95
  1978.7 0.7 fusion.95
  1987.1 0.7 fusion.95
  1988.8 0.7 fusion.95
  1997.3 0.7 fusion.95
  1999.0 0.7 fusion.95
  2000.7 0.7 fusion.95
  2009.2 0.7 fusion.95
  2010.9 0.7 fusion.95
  2019.4 0.7 fusion.95
  2021.1 0.7 fusion.95
  2029.5 0.7 fusion.95
  2031.2 0.7 fusion.95
  2032.9 0.7 fusion.95
  2041.4 0.7 fusion.95
  2043.1 0.7 fusion.95
  2051.6 0.7 fusion.95
  2053.3 0.7 fusion.95
  2061.7 0.7 fusion.95
  2063.4 0.7 fusion.95
  2065.1 0.7 fusion.95
  2073.6 0.7 fusion.95
  2075.3 0.7 fusion.95
  2083.8 0.7 fusion.95
  2085.5 0.7 fusion.95
  2093.9 0.7 fusion.95
  2095.6 0.7 fusion.95
  2097.3 0.7 fusion.95
  2105.8 0.7 fusion.95
  2369.4 3.2 fusion.55
  (5633 shorter events, 1657.2 us)
Async XLA Ops:
  7.2 33.4 %copy-start = (f32[2048,256]{1,0:T(8,128)S(1)}, f32[2048,256]{1,0:T(8,128)}, u32[]{:S(2)}) copy-start(f32[2048,256]{1,0:T(8,128)} %param.10) | copy-start | bytes 6291460
  47.9 45.6 %all-to-all-start = ((f32[16,96,256]{2,1,0:T(8,128)}), f32[16,96,256]{2,1,0:T(8,128)}, u32[]{:S(2)}, u32[]{:S(2)}) async-start(f32[16,96,256]{2,1,0:T(8,128)} %select_multiply_fusion), calls=%async_computation | async-start | bytes 3145728 | tf_op jit(solution)/shard_map/all_to_all | solution.py:76
  57.1 131.7 %all-reduce.4.cloned.1.call-start = ((), (), s32[]{:S(2)}) async-start(), calls=%async_computation.1 | async-start | bytes 524288 | tf_op jit(solution)/shard_map/psum | solution.py:63
  98.3 90.5 %copy-start.2 = (f32[1024,256]{1,0:T(8,128)}, f32[1024,256]{1,0:T(8,128)S(1)}, u32[]{:S(2)}) copy-start(f32[1024,256]{1,0:T(8,128)S(1)} %gather_fusion.2) | copy-start | bytes 3145732
  101.2 1209.3 %all-reduce.6.cloned.1.call-start = ((), (), s32[]{:S(2)}) async-start(), calls=%async_computation.2 | async-start | bytes 524288 | tf_op jit(solution)/shard_map/psum | solution.py:63
  1217.4 1.0 copy-start.1
Sparse Core Ops, SparseCore 0:
  101.3 87.4 all-reduce.3
  1221.1 89.3 all-reduce.5
where the time goes:
time: 2390 us; the launch traced here: 2380 us
  other arithmetic  1050 us (44%)
  local copies, waits for them, and re-layouts  446 us (19%)
  loops' own time  400 us (17%)
  matrix products  241 us (10%)
  waiting for transfers between devices  213 us (9%)
    another operation x2, loops' own time, upper_factor(): lax.fori_loop(0, order_size, column_step, jnp.zeros_like(gram_value))  378 us
    div x512, other arithmetic, row_step(): (unit - jnp.dot(factor_row, solved, precision=highest_precision)) / pivot  367 us
    reduce_sum x512, other arithmetic, column_step(): pivot = jnp.sqrt(jnp.sum(jnp.where(positions == column, residue, 0.0)))  341 us
    reduce_sum x512, other arithmetic, row_step(): pivot = jnp.sum(jnp.where(positions == row, factor_row, 0.0))  327 us
    dynamic_update_slice x512, local copies, waits for them, and re-layouts, column_step(): return lax.dynamic_update_slice_in_dim(lower, entries[:, None], column, 1)  314 us
    psum x2, waiting for transfers between devices, combined_factor(): return upper_factor(lax.psum(local_gram, 'height'))  177 us
    dot_general x512, matrix products, column_step(): residue = target - jnp.dot(lower, row_of, precision=highest_precision)  136 us
    dot_general x512, matrix products, row_step(): jnp.dot(factor_row, solved, precision=highest_precision)  93.5 us

commit v1 on v0

v1 whole, which is shorter than its diff:
```python
import functools

import jax
import jax.numpy as jnp
from jax import lax
from jax.experimental import pallas as pl
from jax.experimental.pallas import tpu as pltpu
from jax.sharding import PartitionSpec as P

BLK = 1024
MAXC = 1536
F32 = jnp.float32
VMEM_LIMIT = 40 * 1024 * 1024


def split3(x):
    high = x.astype(jnp.bfloat16)
    rest = x - high.astype(F32)
    mid = rest.astype(jnp.bfloat16)
    return high, mid, (rest - mid.astype(F32)).astype(jnp.bfloat16)


def dot6(left, right, left_dim, right_dim):
    lh, lm, ll = split3(left)
    rh, rm, rl = split3(right)
    return lax.dot_general(
        jnp.concatenate([ll, lh, lm, lm, lh, lh], left_dim),
        jnp.concatenate([rh, rl, rm, rh, rm, rh], right_dim),
        (((left_dim,), (right_dim,)), ((), ())),
        preferred_element_type=F32,
    )


def two_sum(a, b):
    total = a + b
    part = total - a
    return total, (a - (total - part)) + (b - part)


def power_above(peak):
    power = jnp.full_like(peak, 2.0**-120)
    inverse = jnp.full_like(peak, 2.0**119)
    for step in (100, 64, 32, 16, 8, 4, 2, 1):
        trial = power * 2.0**step
        above = peak >= trial
        power = jnp.where(above, trial, power)
        inverse = jnp.where(above, inverse * 2.0**-step, inverse)
    return power * 2.0, inverse


def slices(x, bits):
    out = []
    for place in bits:
        big = 1.5 * 2.0 ** (23 - place)
        part = (x + big) - big
        out.append(part.astype(jnp.bfloat16))
        x = x - part
    part = x.astype(jnp.bfloat16)
    return out + [part, (x - part.astype(F32)).astype(jnp.bfloat16)]


def gram_pair(n1, n2, n3, n4, *n5):
    n = n1.shape[1]
    dims = (((0,), (0,)), ((), ()))
    d1 = lax.dot_general(n1, jnp.concatenate([n1, n2, n3, n4, *n5], 1), dims, preferred_element_type=F32)
    d2 = lax.dot_general(n2, jnp.concatenate([n2, n3, n4], 1), dims, preferred_element_type=F32)
    d3 = lax.dot_general(n3, n3, dims, preferred_element_type=F32)
    p11, p12, p13, p14 = (d1[:, i * n : (i + 1) * n] for i in range(4))
    p22, p23, p24 = (d2[:, i * n : (i + 1) * n] for i in range(3))
    hi, low1 = two_sum(p11, p12 + p12.T)
    hi, low2 = two_sum(hi, p22 + (p13 + p13.T))
    tail = p14 + p23 + p24
    if n5:
        tail = tail + d1[:, 4 * n :]
    return hi, (low1 + low2) + ((tail + tail.T) + d3)


def column_of(row):
    n = row.shape[1]
    return jnp.broadcast_to(row, (8, n)).T[:, 0:1]


def sweep(work, r_ref, w_ref, b=32, bi=8):
    n = work.shape[0]
    groups = b // 8
    lane = lax.broadcasted_iota(jnp.int32, (8, n), 1)
    sub_wide = lax.broadcasted_iota(jnp.int32, (8, n), 0)
    sub = lax.broadcasted_iota(jnp.int32, (8, 128), 0)

    def wide(x):
        return jnp.concatenate([x] * (n // 128), 1)

    for base in range(0, n, b):
        half = base // 128 * 128
        off = base - half
        own = (lane >= base) & (lane < base + b)
        rows, diag = [], []
        for g in range(groups):
            row = work[base + 8 * g : base + 8 * g + 8, :]
            diag.append(row[:, half : half + 128])
            rows.append(jnp.where(own, jnp.where(lane == base + 8 * g + sub_wide, 1.0, 0.0), row))
        pivots = [jnp.ones((8, 128), F32)] * groups
        for k0 in range(0, b, bi):
            col = {}
            for kk in range(bi):
                for g in range(k0 // 8, groups):
                    at = off + k0 + kk
                    col[kk, g] = jnp.broadcast_to(diag[g][:, at : at + 1], (8, 128))
            for kk in range(bi):
                own_group, s = divmod(k0 + kk, 8)
                pivot = jnp.broadcast_to(col[kk, own_group][s : s + 1, :], (8, 128))
                inverse = 1.0 / pivot
                pivots[own_group] = jnp.where(sub == s, pivot, pivots[own_group])
                mult = {}
                for g in range(own_group, groups):
                    value = col[kk, g] * inverse
                    mult[g] = jnp.where(sub > s, value, 0.0) if g == own_group else value
                for k2 in range(kk + 1, bi):
                    entry = jnp.broadcast_to(col[k2, own_group][s : s + 1, :], (8, 128))
                    for g in range(own_group, groups):
                        col[k2, g] = col[k2, g] - mult[g] * entry
                pivot_row = jnp.broadcast_to(rows[own_group][s : s + 1, :], (8, n))
                pivot_diag = jnp.broadcast_to(diag[own_group][s : s + 1, :], (8, 128))
                for g in range(own_group, groups):
                    rows[g] = rows[g] - wide(mult[g]) * pivot_row
                    diag[g] = diag[g] - mult[g] * pivot_diag
        right, full = [], []
        for g in range(groups):
            scale = lax.rsqrt(pivots[g])
            scale = scale + scale * (0.5 - (0.5 * pivots[g]) * scale * scale)
            scaled = rows[g] * wide(scale)
            own_diag = diag[g] * scale
            blocks = [own_diag if h == half else jnp.zeros((8, 128), F32) for h in range(0, n, 128)]
            upper = own & (lane >= base + 8 * g + sub_wide)
            after = jnp.where(lane >= base + b, scaled, 0.0)
            r_ref[base + 8 * g : base + 8 * g + 8, :] = jnp.where(upper, jnp.concatenate(blocks, 1), after)
            w_ref[base + 8 * g : base + 8 * g + 8, :] = jnp.where(lane < base + b, scaled, 0.0)
            right.append(after)
            full.append(scaled)
        if base + b < n:
            low = (base + b) // 128 * 128
            update = dot6(jnp.concatenate(right, 0)[:, low:], jnp.concatenate(full, 0), 0, 0)
            lanes = lax.broadcasted_iota(jnp.int32, (n - low, n), 1)
            tail = jnp.where((lanes >= base) & (lanes < base + b), 0.0, work[low:, :]) - update
            work = tail if low == 0 else jnp.concatenate([jnp.zeros((low, n), F32), tail], 0)


def block_upper(matrix, b=32):
    n = matrix.shape[0]
    row = lax.broadcasted_iota(jnp.int32, (n, n), 0) // b
    column = lax.broadcasted_iota(jnp.int32, (n, n), 1) // b
    return jnp.where(column < row, 0.0, matrix)


def gram_kernel(row_scale, x_ref, mask_ref, out_ref, a_ref, n1_ref, n2_ref, n3_ref, n4_ref):
    rows, n = x_ref.shape
    peak = jnp.zeros((1, n), F32)
    for c in range(rows // 128):
        keep = jnp.broadcast_to(mask_ref[c : c + 1, :], (128, 128)).T
        keep = jnp.concatenate([keep] * (n // 128), 1)
        chunk = jnp.where(keep > 0, x_ref[c * 128 : c * 128 + 128, :], 0.0)
        a_ref[c * 128 : c * 128 + 128, :] = chunk
        peak = jnp.maximum(peak, jnp.max(jnp.abs(chunk), axis=0, keepdims=True))
    top, shrink = power_above(peak)
    for c in range(rows // 128):
        at = slice(c * 128, c * 128 + 128)
        parts = slices(a_ref[at, :] * shrink, (6, 14, 22))
        for ref, part in zip((n1_ref, n2_ref, n3_ref, n4_ref), parts):
            ref[at, :] = part
    hi, lo = gram_pair(n1_ref[...], n2_ref[...], n3_ref[...], n4_ref[...])
    grow = top * row_scale
    column = column_of(top)
    for index, value in enumerate((hi, lo)):
        value = value * column * grow
        out_ref[index, 0:128, :] = value[0:128, 0:128]
        out_ref[index, 128:256, :] = value[0:128, 128:256]
        out_ref[index, 256:384, :] = value[128:256, 128:256]


def unpack(p):
    a, b, d = p[0:128], p[128:256], p[256:384]
    return jnp.concatenate([jnp.concatenate([a, b], 1), jnp.concatenate([b.T, d], 1)], 0)


def chain_kernel(g_ref, inv_ref, factor_ref, r1, w1, r2, w2):
    hi = unpack(g_ref[0])
    lo = unpack(g_ref[1])
    sweep(block_upper(hi), r1, w1)
    r = r1[...]
    top, shrink = power_above(jnp.max(jnp.abs(r), axis=0, keepdims=True))
    own_hi, own_lo = gram_pair(*slices(r * shrink, (7, 15, 23)))
    column = column_of(top)
    residual = (hi - own_hi * column * top) + (lo - own_lo * column * top)
    w = w1[...]
    near = dot6(w, r, 1, 1)
    gram2 = dot6(near, near, 1, 1) + dot6(dot6(w, residual, 1, 0), w, 1, 1)
    sweep(block_upper(gram2), r2, w2)
    row = lax.broadcasted_iota(jnp.int32, near.shape, 0)
    twice = jnp.where(row == lax.broadcasted_iota(jnp.int32, near.shape, 1), 2.0, 0.0)
    factor_ref[...] = dot6(r2[...], dot6(twice - near, r, 0, 0), 1, 0)
    inv_ref[...] = dot6(w2[...], w, 1, 0)


def compact_kernel(n, slots, stride, own_ref, counts_ref, mask_ref, x_ref, out_ref, rows_ref):
    shift = n.bit_length() - 1
    own = own_ref[0]
    start = lax.fori_loop(0, own, lambda s, total: total + counts_ref[s], jnp.int32(0))
    unroll = 16

    def step(block, rank):
        for u in range(unroll):
            cell = block * unroll + u
            place = ((rank + start) & (n - 1)) * stride + (rank >> shift)
            rows_ref[pl.ds(place, 1), :] = x_ref[pl.ds(cell, 1), :]
            rank = rank + mask_ref[cell]
        return rank

    lax.fori_loop(0, x_ref.shape[0] // unroll, step, jnp.int32(0))

    def copy(c, _):
        at = pl.multiple_of(c * stride, 8)
        out_ref[c] = rows_ref[pl.ds(at, slots), :]
        return 0

    lax.fori_loop(0, n, copy, 0)


def modes_kernel(n, slots, own_ref, counts_ref, recv_ref, inv_ref, out_ref, rows_ref):
    shift = n.bit_length() - 1
    own = own_ref[0]

    def place(s, start):
        first = start + ((own - start) & (n - 1))
        at = first >> shift
        turn = at & 7
        at = pl.multiple_of(at - turn, 8)
        block = pltpu.roll(jnp.concatenate([recv_ref[s], recv_ref[s, 0:8, :]], 0), turn, 0)
        head = lax.broadcasted_iota(jnp.int32, (8, block.shape[1]), 0) < turn
        rows_ref[pl.ds(at, 8), :] = jnp.where(head, rows_ref[pl.ds(at, 8), :], block[0:8])
        rows_ref[pl.ds(at + 8, slots), :] = block[8:]
        return start + counts_ref[s]

    lax.fori_loop(0, n, place, jnp.int32(0))
    out_ref[...] = dot6(rows_ref[0 : out_ref.shape[0], :], inv_ref[...], 1, 1)


VMEM = pl.BlockSpec(memory_space=pltpu.VMEM)
SMEM = pl.BlockSpec(memory_space=pltpu.SMEM)


def call(kernel, name, out, in_specs, scratch, flops, args):
    return pl.pallas_call(
        kernel,
        name=name,
        out_shape=out,
        in_specs=in_specs,
        out_specs=jax.tree.map(lambda _: VMEM, out),
        scratch_shapes=scratch,
        compiler_params=pltpu.CompilerParams(vmem_limit_bytes=VMEM_LIMIT),
        cost_estimate=pl.CostEstimate(flops=flops, bytes_accessed=4 << 20, transcendentals=0),
    )(*args)


def reduce_pair(pair, n, own):
    def other(x, bit):
        return lax.ppermute(x, "height", [(i, i ^ bit) for i in range(n)])

    def add(a, b):
        total, error = two_sum(a[0], b[0])
        return jnp.stack([total, (a[1] + b[1]) + error])

    halved = [1, 2]
    for bit in halved:
        size = pair.shape[1] // 2
        mine = jnp.where((own & bit) > 0, size, 0)
        sent = lax.dynamic_slice_in_dim(pair, size - mine, size, 1)
        pair = add(lax.dynamic_slice_in_dim(pair, mine, size, 1), other(sent, bit))
    bit = 4
    while bit < n:
        pair = add(pair, other(pair, bit))
        bit *= 2
    for bit in halved[::-1]:
        got = other(pair, bit)
        high = (own & bit) > 0
        pair = jnp.concatenate([jnp.where(high, got, pair), jnp.where(high, pair, got)], 1)
    return pair


def local(snapshots, fluid_mask):
    n = lax.axis_size("height")
    own = lax.axis_index("height")
    cells, k = snapshots.shape
    slots = (-(-MAXC // n) + 7) // 8 * 8
    stride = slots + 8
    own_list = own.reshape(1)

    pair = call(
        functools.partial(gram_kernel, 1.0 / (n * BLK)),
        "gram",
        jax.ShapeDtypeStruct((2, 384, 128), F32),
        [VMEM, VMEM],
        [pltpu.VMEM((cells, k), F32)] + [pltpu.VMEM((cells, k), jnp.bfloat16)] * 4,
        16 * cells * k * k,
        (snapshots, fluid_mask.reshape(cells // 128, 128)),
    )
    counts = jnp.where(jnp.arange(n) == own, jnp.sum(fluid_mask), 0)
    bit = 1
    while bit < n:
        counts = counts + lax.ppermute(counts, "height", [(i, i ^ bit) for i in range(n)])
        bit *= 2
    outgoing = call(
        functools.partial(compact_kernel, n, slots, stride),
        "compact",
        jax.ShapeDtypeStruct((n, slots, k), F32),
        [SMEM, SMEM, SMEM, VMEM],
        [pltpu.VMEM((n * stride, k), F32)],
        1 << 30,
        (own_list, counts, fluid_mask, snapshots),
    )
    received = lax.all_to_all(outgoing, "height", split_axis=0, concat_axis=0, tiled=True)
    pair = reduce_pair(pair, n, own)
    square = jax.ShapeDtypeStruct((k, k), F32)
    inverse, factor = call(
        chain_kernel,
        "chain",
        [square, square],
        [VMEM],
        [pltpu.VMEM((k, k), F32)] * 4,
        20 << 30,
        (pair,),
    )
    modes = call(
        functools.partial(modes_kernel, n, slots),
        "modes",
        jax.ShapeDtypeStruct((BLK, k), F32),
        [SMEM, SMEM, VMEM, VMEM],
        [pltpu.VMEM((BLK + slots + 8, k), F32)],
        12 * BLK * k * k,
        (own_list, counts, received, inverse),
    )
    return (modes, factor)


def solution(mesh):
    return jax.shard_map(
        local,
        mesh=mesh,
        in_specs=(P(("parts", "height"), None), P(("parts", "height"))),
        out_specs=(P(("parts", "height"), None), P("parts", None)),
        check_vma=False,
    )
```

time: 2390 us -> 88.5 us (0.04)
  other arithmetic: 1050 us -> 2.82 us
  local copies, waits for them, and re-layouts: 446 us -> 2.31 us
  loops' own time: 400 us -> 0 us
  matrix products: 241 us -> 0 us
  waiting for transfers between devices: 213 us -> 27.4 us
  Pallas kernels: 0 us -> 39.4 us
    reduce_sum x1027 -> x1, other arithmetic: 670 us -> 0.63 us  [local(): counts = jnp.where(jnp.arange(n) == own, jnp.sum(fluid_mask), 0)]
    another operation x4 -> x0, loops' own time: 400 us -> none  [the longest x2 378 us: upper_factor(): lax.fori_loop(0, order_size, column_step, jnp.zeros_like(gram_value))]
    div x512 -> x0, other arithmetic: 367 us -> none  [row_step(): (unit - jnp.dot(factor_row, solved, precision=highest_precision)) / pivot]
    dynamic_update_slice x1024 -> x0, local copies, waits for them, and re-layouts: 336 us -> none  [the longest x512 314 us: column_step(): return lax.dynamic_update_slice_in_dim(lower, entries[:, None], column, 1)]
    dot_general x1029 -> x0, matrix products: 241 us -> none  [the longest x512 136 us: column_step(): residue = target - jnp.dot(lower, row_of, precision=highest_precision)]
    psum x2 -> x0, waiting for transfers between devices: 177 us -> none  [combined_factor(): return upper_factor(lax.psum(local_gram, 'height'))]
    broadcast_in_dim x512 -> x0, local copies, waits for them, and re-layouts: 68.4 us -> none  [column_step(): return lax.dynamic_update_slice_in_dim(lower, entries[:, None], column, 1)]
    pallas_call x0 -> x4, Pallas kernels: none -> 39.4 us  [call(): pl.pallas_call(kernel, name=name, out_shape=out, in_specs=in_specs, out_s...]
where the time goes in v1:
time: 88.5 us; the launch traced here: 88.2 us
  Pallas kernels  39.4 us (45%)
  waiting for transfers between devices  27.4 us (31%)
  starting transfers between devices  15.5 us (18%)
  other arithmetic  2.82 us (3%)
  local copies, waits for them, and re-layouts  2.31 us (3%)
    pallas_call x4, Pallas kernels, call(): pl.pallas_call(kernel, name=name, out_shape=out, in_specs=in_specs, out_s...  39.4 us
    all_to_all x1, waiting for transfers between devices, local(): lax.all_to_all(outgoing, 'height', split_axis=0, concat_axis=0, tiled=True)  15.7 us
    all_to_all x1, starting transfers between devices, local(): lax.all_to_all(outgoing, 'height', split_axis=0, concat_axis=0, tiled=True)  9.76 us
    ppermute x6, waiting for transfers between devices, other(): return lax.ppermute(x, 'height', [(i, i ^ bit) for i in range(n)])  6.18 us
    ppermute x4, waiting for transfers between devices, local(): lax.ppermute(counts, 'height', [(i, i ^ bit) for i in range(n)])  5.46 us
    ppermute x6, starting transfers between devices, other(): return lax.ppermute(x, 'height', [(i, i ^ bit) for i in range(n)])  4.36 us
    unnamed x8, local copies, waits for them, and re-layouts  2.29 us
  transfers between devices with their start and end apart: 11, of which 7 were waited for; matrix products, arithmetic and copies ran while one was open for 3% of the time, Pallas kernels for 37%

profile of v1, /device:TPU:13, one launch (start us, length us, event | category | flops | bytes accessed | tf_op | source)
XLA Modules:
  0.0 88.2 jit_solution(2353149734510659504)
XLA Ops:
  0.6 0.0 copy-start
  0.6 0.7 copy-done
  1.3 0.0 copy-start.2
  1.3 1.6 %copy-done.2 = f32[2048,256]{1,0:T(8,128)S(1)} copy-done((f32[2048,256]{1,0:T(8,128)S(1)}, f32[2048,256]{1,0:T(8,128)}, u32[]{:S(2)}) %copy-start.2) | copy-done | bytes 2097176
  2.9 0.0 copy-start.1
  2.9 3.8 %gram.1 = f32[2,384,128]{2,1,0:T(8,128)S(1)} custom-call(f32[2048,256]{1,0:T(8,128)S(1)} %copy-done.2, s32[16,128]{1,0:T(8,128)S(1)} %bitcast.2), custom_call_target="tpu_custom_call" | custom-call | flops 2147483648 | bytes 4194304 | tf_op jit(solution)/shard_map/gram/pallas_call | solution.py:252
  6.7 0.0 copy-start.3
  6.7 0.7 collective-permute-start.4
  7.5 0.0 copy-done.1
  7.5 0.6 reduce_sum.9
  8.1 0.4 collective-permute-done.4
  8.6 0.3 collective-permute-start.5
  8.9 0.6 compare_select_fusion
  9.6 0.7 collective-permute-start
  10.3 2.4 %collective-permute-done.5 = f32[2,96,128]{2,1,0:T(8,128)S(1)} collective-permute-done((f32[2,96,128]{2,1,0:T(8,128)S(1)}, f32[2,96,128]{2,1,0:T(8,128)S(1)}, u32[]{:S(2)}, u32[]{:S(2)}) %collective-permute-start.5) | collective-permute-done | bytes 98336 | tf_op jit(solution)/shard_map/ppermute | solution.py:266
  12.7 0.2 collective-permute-start.6
  13.0 0.0 collective-permute-done
  13.0 0.6 fusion.6
  13.6 0.4 collective-permute-start.1
  14.0 2.2 %collective-permute-done.6 = f32[2,96,128]{2,1,0:T(8,128)S(1)} collective-permute-done((f32[2,96,128]{2,1,0:T(8,128)S(1)}, f32[2,96,128]{2,1,0:T(8,128)S(1)}, u32[]{:S(2)}, u32[]{:S(2)}) %collective-permute-start.6) | collective-permute-done | bytes 98336 | tf_op jit(solution)/shard_map/ppermute | solution.py:266
  16.3 2.4 %collective-permute-start.7 = (f32[2,96,128]{2,1,0:T(8,128)S(1)}, f32[2,96,128]{2,1,0:T(8,128)S(1)}, u32[]{:S(2)}, u32[]{:S(2)}) collective-permute-start(f32[2,96,128]{2,1,0:T(8,128)S(1)} %pad_maximum_fusion.3), channel_id=1, source_target_pairs={{0,8},{1,9},{2,10},{3,11},{4,12},{5,13},{6,14},{7,15},{8,0},{9,1},... | collective-permute-start | bytes 294920 | tf_op jit(solution)/shard_map/ppermute | solution.py:266
  18.7 0.0 collective-permute-done.1
  18.7 0.7 fusion.7
  19.3 0.2 collective-permute-start.2
  19.6 2.2 %collective-permute-done.2 = s32[16]{0:T(128)S(1)} collective-permute-done((s32[16]{0:T(128)S(1)}, s32[16]{0:T(128)S(1)}, u32[]{:S(2)}, u32[]{:S(2)}) %collective-permute-start.2) | collective-permute-done | bytes 96 | tf_op jit(solution)/shard_map/ppermute | solution.py:309
  21.8 0.1 collective-permute-start.3
  21.9 3.2 %collective-permute-done.3 = s32[16]{0:T(128)S(1)} collective-permute-done((s32[16]{0:T(128)S(1)}, s32[16]{0:T(128)S(1)}, u32[]{:S(2)}, u32[]{:S(2)}) %collective-permute-start.3) | collective-permute-done | bytes 96 | tf_op jit(solution)/shard_map/ppermute | solution.py:309
  25.1 0.0 collective-permute-done.7
  25.1 0.3 collective-permute-start.8
  25.4 0.0 copy-done.3
  25.4 13.7 %compact.1 = f32[16,96,256]{2,1,0:T(8,128)} custom-call(s32[1]{0:T(128)} %bitcast.own_ref, s32[16]{0:T(128)S(1)} %add.108.counts_ref, s32[2048]{0:T(1024)S(1)} %copy-done.1, f32[2048,256]{1,0:T(8,128)S(1)} %copy-done.3), custom_call_target="tpu_custom_call" | custom-call | flops 1073741824 | bytes 4194304 | tf_op jit(solution)/shard_map/compact/pallas_call | solution.py:252
  39.2 9.8 %all-to-all-start = ((f32[16,96,256]{2,1,0:T(8,128)}), f32[16,96,256]{2,1,0:T(8,128)S(1)}, u32[]{:S(2)}, u32[]{:S(2)}) async-start(f32[16,96,256]{2,1,0:T(8,128)} %compact.1), calls=%async_computation | async-start | bytes 3145728 | tf_op jit(solution)/shard_map/all_to_all | solution.py:320
  48.9 0.0 collective-permute-done.8
  49.0 0.4 collective-permute-start.9
  49.4 1.1 %collective-permute-done.9 = f32[2,192,128]{2,1,0:T(8,128)S(1)} collective-permute-done((f32[2,192,128]{2,1,0:T(8,128)S(1)}, f32[2,192,128]{2,1,0:T(8,128)S(1)}, u32[]{:S(2)}, u32[]{:S(2)}) %collective-permute-start.9) | collective-permute-done | bytes 196640 | tf_op jit(solution)/shard_map/ppermute | solution.py:266
  50.6 18.8 %chain.1 = (f32[256,256]{1,0:T(8,128)S(1)}, f32[256,256]{1,0:T(8,128)}) custom-call(f32[2,384,128]{2,1,0:T(8,128)S(1)} %pad_maximum_fusion.g_ref), custom_call_target="tpu_custom_call" | custom-call | flops 21474836480 | bytes 4194304 | tf_op jit(solution)/shard_map/chain/pallas_call | solution.py:252
  69.4 15.7 %all-to-all-done.recv_ref = f32[16,96,256]{2,1,0:T(8,128)S(1)} async-done(((f32[16,96,256]{2,1,0:T(8,128)}), f32[16,96,256]{2,1,0:T(8,128)S(1)}, u32[]{:S(2)}, u32[]{:S(2)}) %all-to-all-start) | async-done | bytes 1572896 | tf_op jit(solution)/shard_map/all_to_all | solution.py:320
  85.1 3.1 %modes.1 = f32[1024,256]{1,0:T(8,128)} custom-call(s32[1]{0:T(128)} %bitcast.own_ref, s32[16]{0:T(128)S(1)} %add.108.counts_ref, f32[16,96,256]{2,1,0:T(8,128)S(1)} %all-to-all-done.recv_ref, f32[256,256]{1,0:T(8,128)S(1)} %get-tuple-element.4.inv_ref), custom_call_target="tpu_custom_call" | custom-call | flops 805306368 | bytes 4194304 | tf_op jit(solution)/shard_map/modes/pallas_call | solution.py:252
  (15 shorter events, 0.3 us)
Async XLA Ops:
  0.6 0.7 copy-start
  1.3 1.6 %copy-start.2 = (f32[2048,256]{1,0:T(8,128)S(1)}, f32[2048,256]{1,0:T(8,128)}, u32[]{:S(2)}) copy-start(f32[2048,256]{1,0:T(8,128)} %x_ref.3) | copy-start | bytes 6291460
  2.9 4.5 %copy-start.1 = (s32[2048]{0:T(1024)S(1)}, s32[2048]{0:T(1024)}, u32[]{:S(2)}) copy-start(s32[2048]{0:T(1024)} %mask_ref.1) | copy-start | bytes 24580
  6.7 18.7 %copy-start.3 = (f32[2048,256]{1,0:T(8,128)S(1)}, f32[2048,256]{1,0:T(8,128)}, u32[]{:S(2)}) copy-start(f32[2048,256]{1,0:T(8,128)} %x_ref.3) | copy-start | bytes 6291460
  6.7 1.8 %collective-permute-start.4 = (f32[2,192,128]{2,1,0:T(8,128)S(1)}, f32[2,192,128]{2,1,0:T(8,128)S(1)}, u32[]{:S(2)}, u32[]{:S(2)}) collective-permute-start(f32[2,192,128]{2,1,0:T(8,128)S(1)} %constant_dynamic-slice_fusion), channel_id=1, source_target_pairs={{0,1},{1,0},{2,3},{3,2},{4,5},{5,4},{6,7},{7,6},{8,9},{9,8},{10,11... | collective-permute-start | bytes 589832 | tf_op jit(solution)/shard_map/ppermute | solution.py:266
  8.6 4.1 %collective-permute-start.5 = (f32[2,96,128]{2,1,0:T(8,128)S(1)}, f32[2,96,128]{2,1,0:T(8,128)S(1)}, u32[]{:S(2)}, u32[]{:S(2)}) collective-permute-start(f32[2,96,128]{2,1,0:T(8,128)S(1)} %get-tuple-element.17), channel_id=1, source_target_pairs={{0,2},{1,3},{2,0},{3,1},{4,6},{5,7},{6,4},{7,5},{8,10},{9,11},{10,... | collective-permute-start | bytes 294920 | tf_op jit(solution)/shard_map/ppermute | solution.py:266
  9.6 3.4 %collective-permute-start = (s32[16]{0:T(128)S(1)}, s32[16]{0:T(128)S(1)}, u32[]{:S(2)}, u32[]{:S(2)}) collective-permute-start(s32[16]{0:T(128)S(1)} %compare_select_fusion), channel_id=1, source_target_pairs={{0,1},{1,0},{2,3},{3,2},{4,5},{5,4},{6,7},{7,6},{8,9},{9,8},{10,11... | collective-permute-start | bytes 200 | tf_op jit(solution)/shard_map/ppermute | solution.py:309
  12.7 3.5 %collective-permute-start.6 = (f32[2,96,128]{2,1,0:T(8,128)S(1)}, f32[2,96,128]{2,1,0:T(8,128)S(1)}, u32[]{:S(2)}, u32[]{:S(2)}) collective-permute-start(f32[2,96,128]{2,1,0:T(8,128)S(1)} %pad_maximum_fusion.2), channel_id=1, source_target_pairs={{0,4},{1,5},{2,6},{3,7},{4,0},{5,1},{6,2},{7,3},{8,12},{9,13},{10,... | collective-permute-start | bytes 294920 | tf_op jit(solution)/shard_map/ppermute | solution.py:266
  13.6 5.1 %collective-permute-start.1 = (s32[16]{0:T(128)S(1)}, s32[16]{0:T(128)S(1)}, u32[]{:S(2)}, u32[]{:S(2)}) collective-permute-start(s32[16]{0:T(128)S(1)} %fusion.6), channel_id=1, source_target_pairs={{0,2},{1,3},{2,0},{3,1},{4,6},{5,7},{6,4},{7,5},{8,10},{9,11},{10,... | collective-permute-start | bytes 200 | tf_op jit(solution)/shard_map/ppermute | solution.py:309
  16.3 8.8 %collective-permute-start.7 = (f32[2,96,128]{2,1,0:T(8,128)S(1)}, f32[2,96,128]{2,1,0:T(8,128)S(1)}, u32[]{:S(2)}, u32[]{:S(2)}) collective-permute-start(f32[2,96,128]{2,1,0:T(8,128)S(1)} %pad_maximum_fusion.3), channel_id=1, source_target_pairs={{0,8},{1,9},{2,10},{3,11},{4,12},{5,13},{6,14},{7,15},{8,0},{9,1},... | collective-permute-start | bytes 294920 | tf_op jit(solution)/shard_map/ppermute | solution.py:266
  19.3 2.5 %collective-permute-start.2 = (s32[16]{0:T(128)S(1)}, s32[16]{0:T(128)S(1)}, u32[]{:S(2)}, u32[]{:S(2)}) collective-permute-start(s32[16]{0:T(128)S(1)} %fusion.7), channel_id=1, source_target_pairs={{0,4},{1,5},{2,6},{3,7},{4,0},{5,1},{6,2},{7,3},{8,12},{9,13},{10,... | collective-permute-start | bytes 200 | tf_op jit(solution)/shard_map/ppermute | solution.py:309
  21.8 3.3 %collective-permute-start.3 = (s32[16]{0:T(128)S(1)}, s32[16]{0:T(128)S(1)}, u32[]{:S(2)}, u32[]{:S(2)}) collective-permute-start(s32[16]{0:T(128)S(1)} %add.107), channel_id=1, source_target_pairs={{0,8},{1,9},{2,10},{3,11},{4,12},{5,13},{6,14},{7,15},{8,0},{9,1},... | collective-permute-start | bytes 200 | tf_op jit(solution)/shard_map/ppermute | solution.py:309
  25.1 23.8 %collective-permute-start.8 = (f32[2,96,128]{2,1,0:T(8,128)S(1)}, f32[2,96,128]{2,1,0:T(8,128)S(1)}, u32[]{:S(2)}, u32[]{:S(2)}) collective-permute-start(f32[2,96,128]{2,1,0:T(8,128)S(1)} %pad_maximum_fusion.4), channel_id=1, source_target_pairs={{0,2},{1,3},{2,0},{3,1},{4,6},{5,7},{6,4},{7,5},{8,10},{9,11},{10,... | collective-permute-start | bytes 294920 | tf_op jit(solution)/shard_map/ppermute | solution.py:266
  39.2 46.0 %all-to-all-start = ((f32[16,96,256]{2,1,0:T(8,128)}), f32[16,96,256]{2,1,0:T(8,128)S(1)}, u32[]{:S(2)}, u32[]{:S(2)}) async-start(f32[16,96,256]{2,1,0:T(8,128)} %compact.1), calls=%async_computation | async-start | bytes 3145728 | tf_op jit(solution)/shard_map/all_to_all | solution.py:320
  49.0 1.5 %collective-permute-start.9 = (f32[2,192,128]{2,1,0:T(8,128)S(1)}, f32[2,192,128]{2,1,0:T(8,128)S(1)}, u32[]{:S(2)}, u32[]{:S(2)}) collective-permute-start(f32[2,192,128]{2,1,0:T(8,128)S(1)} %pad_maximum_fusion.1), channel_id=1, source_target_pairs={{0,1},{1,0},{2,3},{3,2},{4,5},{5,4},{6,7},{7,6},{8,9},{9,8},{10,11... | collective-permute-start | bytes 589832 | tf_op jit(solution)/shard_map/ppermute | solution.py:266

commit v2 on v1

--- a/solution.py
+++ b/solution.py
@@ -35,6 +35,11 @@
     total = a + b
     part = total - a
     return total, (a - (total - part)) + (b - part)
+
+
+def add_pair(a, b):
+    total, error = two_sum(a[0], b[0])
+    return total, (a[1] + b[1]) + error
 
 
 def power_above(peak):
@@ -152,29 +157,49 @@
     return jnp.where(column < row, 0.0, matrix)
 
 
-def gram_kernel(row_scale, x_ref, mask_ref, out_ref, a_ref, n1_ref, n2_ref, n3_ref, n4_ref):
+def gram_kernel(row_scale, own_ref, x_ref, mask_ref, keep_ref, send_ref, a_ref, n1_ref, n2_ref, n3_ref, n4_ref):
     rows, n = x_ref.shape
-    peak = jnp.zeros((1, n), F32)
+    peak = jnp.zeros((8, n), F32)
     for c in range(rows // 128):
         keep = jnp.broadcast_to(mask_ref[c : c + 1, :], (128, 128)).T
         keep = jnp.concatenate([keep] * (n // 128), 1)
         chunk = jnp.where(keep > 0, x_ref[c * 128 : c * 128 + 128, :], 0.0)
         a_ref[c * 128 : c * 128 + 128, :] = chunk
-        peak = jnp.maximum(peak, jnp.max(jnp.abs(chunk), axis=0, keepdims=True))
-    top, shrink = power_above(peak)
+        peak = jnp.maximum(peak, jnp.max(jnp.abs(chunk).reshape(16, 8, n), axis=0))
+    top, shrink = power_above(jnp.max(peak, axis=0, keepdims=True))
     for c in range(rows // 128):
         at = slice(c * 128, c * 128 + 128)
-        parts = slices(a_ref[at, :] * shrink, (6, 14, 22))
-        for ref, part in zip((n1_ref, n2_ref, n3_ref, n4_ref), parts):
+        for ref, part in zip((n1_ref, n2_ref, n3_ref, n4_ref), slices(a_ref[at, :] * shrink, (6, 14, 22))):
             ref[at, :] = part
-    hi, lo = gram_pair(n1_ref[...], n2_ref[...], n3_ref[...], n4_ref[...])
-    grow = top * row_scale
-    column = column_of(top)
-    for index, value in enumerate((hi, lo)):
+    pair = gram_pair(n1_ref[...], n2_ref[...], n3_ref[...], n4_ref[...])
+    column, grow = column_of(top), top * row_scale
+    odd = (own_ref[0] & 1) > 0
+    live = jnp.sum(mask_ref[...].astype(F32), axis=(0, 1), keepdims=True)
+    lane = lax.broadcasted_iota(jnp.int32, (8, 128), 1)
+    count = jnp.where(lane == own_ref[0], live, 0.0)
+    for index, value in enumerate(pair):
         value = value * column * grow
-        out_ref[index, 0:128, :] = value[0:128, 0:128]
-        out_ref[index, 128:256, :] = value[0:128, 128:256]
-        out_ref[index, 256:384, :] = value[128:256, 128:256]
+        blocks = (value[0:128, 0:128], value[0:128, 128:256], value[128:256, 128:256])
+        first = jnp.concatenate([blocks[0], blocks[1][0:64]], 0)
+        second = jnp.concatenate([blocks[1][64:128], blocks[2]], 0)
+        size = first.shape[0]
+        keep_ref[index, 0:size] = jnp.where(odd, second, first)
+        send_ref[index, 0:size] = jnp.where(odd, first, second)
+        for ref in (keep_ref, send_ref):
+            ref[index, size:] = count if index == 0 else jnp.zeros_like(count)
+
+
+def quarter_kernel(own_ref, keep_ref, got_ref, mine_ref, *send_refs):
+    size = mine_ref.shape[1] - 8
+    place = (own_ref[0] >> 1) & 3
+    for turn, ref in enumerate((mine_ref,) + send_refs):
+        for to, at in (
+            (pl.ds(0, size), pl.ds(pl.multiple_of((place ^ turn) * size, 8), size)),
+            (pl.ds(size, 8), pl.ds(4 * size, 8)),
+        ):
+            ref[0, to, :], ref[1, to, :] = add_pair(
+                (keep_ref[0, at, :], keep_ref[1, at, :]), (got_ref[0, at, :], got_ref[1, at, :])
+            )
 
 
 def unpack(p):
@@ -182,9 +207,12 @@
     return jnp.concatenate([jnp.concatenate([a, b], 1), jnp.concatenate([b.T, d], 1)], 0)
 
 
-def chain_kernel(g_ref, inv_ref, factor_ref, r1, w1, r2, w2):
-    hi = unpack(g_ref[0])
-    lo = unpack(g_ref[1])
+def chain_kernel(own_ref, half_ref, got_ref, inv_ref, factor_ref, r1, w1, r2, w2):
+    odd = (own_ref[0] & 1) > 0
+    hi, lo = (
+        unpack(jnp.concatenate([jnp.where(odd, got, half), jnp.where(odd, half, got)], 0))
+        for half, got in ((half_ref[0], got_ref[0]), (half_ref[1], got_ref[1]))
+    )
     sweep(block_upper(hi), r1, w1)
     r = r1[...]
     top, shrink = power_above(jnp.max(jnp.abs(r), axis=0, keepdims=True))
@@ -201,31 +229,51 @@
     inv_ref[...] = dot6(w2[...], w, 1, 0)
 
 
-def compact_kernel(n, slots, stride, own_ref, counts_ref, mask_ref, x_ref, out_ref, rows_ref):
+def compact_kernel(n, starts_ref, mask_ref, x_ref, out_ref, rank_ref):
+    slots = out_ref.shape[1]
     shift = n.bit_length() - 1
-    own = own_ref[0]
-    start = lax.fori_loop(0, own, lambda s, total: total + counts_ref[s], jnp.int32(0))
-    unroll = 16
-
-    def step(block, rank):
-        for u in range(unroll):
-            cell = block * unroll + u
-            place = ((rank + start) & (n - 1)) * stride + (rank >> shift)
-            rows_ref[pl.ds(place, 1), :] = x_ref[pl.ds(cell, 1), :]
-            rank = rank + mask_ref[cell]
-        return rank
-
-    lax.fori_loop(0, x_ref.shape[0] // unroll, step, jnp.int32(0))
-
-    def copy(c, _):
-        at = pl.multiple_of(c * stride, 8)
-        out_ref[c] = rows_ref[pl.ds(at, slots), :]
+    width = 16
+    blocks = mask_ref.shape[0]
+    live = mask_ref[...]
+    before = lax.broadcasted_iota(jnp.int32, (128, 128), 0) < lax.broadcasted_iota(jnp.int32, (128, 128), 1)
+    rank_ref[...] = jnp.dot(
+        live.astype(F32).astype(jnp.bfloat16),
+        jnp.where(before, 1.0, 0.0).astype(jnp.bfloat16),
+        preferred_element_type=F32,
+    ).astype(jnp.int32)
+    out_ref[...] = jnp.zeros_like(out_ref)
+    row = lax.broadcasted_iota(jnp.int32, (n * width, 128), 0)
+
+    def step(b, _):
+        first = starts_ref[b]
+        low = pl.multiple_of(jnp.minimum((first >> shift) & -8, slots - width), 8)
+        rank = rank_ref[pl.ds(b, 1), :] + first
+        target = (rank & (n - 1)) * width + (rank >> shift) - low
+        target = jnp.where(mask_ref[pl.ds(b, 1), :] > 0, target, -1)
+        pick = jnp.where(row == target, 1.0, 0.0).astype(jnp.bfloat16)
+        cells = x_ref[pl.ds(pl.multiple_of(b * 128, 128), 128), :]
+        moved = jnp.dot(
+            jnp.concatenate([pick] * 3, 1), jnp.concatenate(split3(cells), 0), preferred_element_type=F32
+        )
+        for c in range(n):
+            out_ref[c, pl.ds(low, width), :] += moved[c * width : c * width + width]
         return 0
 
-    lax.fori_loop(0, n, copy, 0)
-
-
-def modes_kernel(n, slots, own_ref, counts_ref, recv_ref, inv_ref, out_ref, rows_ref):
+    lax.fori_loop(0, blocks, step, 0, unroll=4 if n <= 16 else 1)
+
+
+def turn_kernel(n, own_ref, counts_ref, blocks_ref, out_ref, sem):
+    start = lax.fori_loop(0, own_ref[0], lambda s, total: total + counts_ref[s], jnp.int32(0))
+    copies = [
+        pltpu.make_async_copy(blocks_ref.at[(d - start) & (n - 1)], out_ref.at[d], sem.at[d]) for d in range(n)
+    ]
+    for copy in copies:
+        copy.start()
+    for copy in copies:
+        copy.wait()
+
+
+def modes_kernel(n, slots, own_ref, counts_ref, recv_ref, inv_ref, out_ref, rows_ref, done_ref, sem):
     shift = n.bit_length() - 1
     own = own_ref[0]
 
@@ -241,49 +289,56 @@
         return start + counts_ref[s]
 
     lax.fori_loop(0, n, place, jnp.int32(0))
-    out_ref[...] = dot6(rows_ref[0 : out_ref.shape[0], :], inv_ref[...], 1, 1)
+    step = out_ref.shape[0] // sem.shape[0]
+    copies = []
+    for c in range(sem.shape[0]):
+        at = pl.ds(c * step, step)
+        done_ref[at, :] = dot6(rows_ref[at, :], inv_ref[...], 1, 1)
+        copies.append(pltpu.make_async_copy(done_ref.at[at], out_ref.at[at], sem.at[c]))
+        copies[-1].start()
+    for copy in copies:
+        copy.wait()
 
 
 VMEM = pl.BlockSpec(memory_space=pltpu.VMEM)
 SMEM = pl.BlockSpec(memory_space=pltpu.SMEM)
-
-
-def call(kernel, name, out, in_specs, scratch, flops, args):
+HBM = pl.BlockSpec(memory_space=pltpu.HBM)
+
+
+def call(kernel, name, out, in_specs, scratch, flops, args, out_space=VMEM):
     return pl.pallas_call(
         kernel,
         name=name,
         out_shape=out,
         in_specs=in_specs,
-        out_specs=jax.tree.map(lambda _: VMEM, out),
+        out_specs=jax.tree.map(lambda _: out_space, out),
         scratch_shapes=scratch,
         compiler_params=pltpu.CompilerParams(vmem_limit_bytes=VMEM_LIMIT),
         cost_estimate=pl.CostEstimate(flops=flops, bytes_accessed=4 << 20, transcendentals=0),
     )(*args)
 
 
-def reduce_pair(pair, n, own):
-    def other(x, bit):
-        return lax.ppermute(x, "height", [(i, i ^ bit) for i in range(n)])
-
-    def add(a, b):
-        total, error = two_sum(a[0], b[0])
-        return jnp.stack([total, (a[1] + b[1]) + error])
-
-    halved = [1, 2]
-    for bit in halved:
-        size = pair.shape[1] // 2
-        mine = jnp.where((own & bit) > 0, size, 0)
-        sent = lax.dynamic_slice_in_dim(pair, size - mine, size, 1)
-        pair = add(lax.dynamic_slice_in_dim(pair, mine, size, 1), other(sent, bit))
-    bit = 4
-    while bit < n:
-        pair = add(pair, other(pair, bit))
-        bit *= 2
-    for bit in halved[::-1]:
-        got = other(pair, bit)
-        high = (own & bit) > 0
-        pair = jnp.concatenate([jnp.where(high, got, pair), jnp.where(high, pair, got)], 1)
-    return pair
+def other(x, bits, n):
+    return lax.ppermute(x, "height", [(i, i ^ bits) for i in range(n)])
+
+
+def add(a, b):
+    return jnp.stack(add_pair(a, b))
+
+
+def gather_quarters(mine, n):
+    return [mine] + [other(mine, 2 * turn, n) for turn in (3, 2, 1)][::-1]
+
+
+def assemble(got, own):
+    place = (own >> 1) & 3
+    return jnp.concatenate(
+        [
+            jnp.where(place < 2, *(jnp.where((place & 1) > 0, got[c ^ h ^ 1], got[c ^ h]) for h in (0, 2)))
+            for c in range(4)
+        ],
+        1,
+    )
 
 
 def local(snapshots, fluid_mask):
@@ -291,52 +346,77 @@
     own = lax.axis_index("height")
     cells, k = snapshots.shape
     slots = (-(-MAXC // n) + 7) // 8 * 8
-    stride = slots + 8
     own_list = own.reshape(1)
-
-    pair = call(
+    mask = fluid_mask.reshape(cells // 128, 128)
+    block = jnp.arange(cells // 128)
+    starts = jnp.sum(jnp.where(block[None, :, None] < block[:, None, None], mask[None], 0), (1, 2))
+    half = jax.ShapeDtypeStruct((2, 200, 128), F32)
+    keep, send = call(
         functools.partial(gram_kernel, 1.0 / (n * BLK)),
         "gram",
-        jax.ShapeDtypeStruct((2, 384, 128), F32),
-        [VMEM, VMEM],
+        [half, half],
+        [SMEM, VMEM, VMEM],
         [pltpu.VMEM((cells, k), F32)] + [pltpu.VMEM((cells, k), jnp.bfloat16)] * 4,
         16 * cells * k * k,
-        (snapshots, fluid_mask.reshape(cells // 128, 128)),
-    )
-    counts = jnp.where(jnp.arange(n) == own, jnp.sum(fluid_mask), 0)
-    bit = 1
-    while bit < n:
-        counts = counts + lax.ppermute(counts, "height", [(i, i ^ bit) for i in range(n)])
-        bit *= 2
-    outgoing = call(
-        functools.partial(compact_kernel, n, slots, stride),
+        (own_list, snapshots, mask),
+    )
+    size = keep.shape[1] // 4 // 8 * 8
+    quarter = jax.ShapeDtypeStruct((2, size + 8, 128), F32)
+    mine, side, up, across = call(
+        quarter_kernel, "quarter", [quarter] * 4, [SMEM, VMEM, VMEM], [], 1 << 20, (own_list, keep, other(send, 1, n))
+    )
+    got = [other(across, 6, n), other(up, 4, n), other(side, 2, n)]
+    starts, mine = lax.optimization_barrier((starts, mine))
+    blocks = call(
+        functools.partial(compact_kernel, n),
         "compact",
         jax.ShapeDtypeStruct((n, slots, k), F32),
-        [SMEM, SMEM, SMEM, VMEM],
-        [pltpu.VMEM((n * stride, k), F32)],
-        1 << 30,
-        (own_list, counts, fluid_mask, snapshots),
-    )
+        [SMEM, VMEM, VMEM],
+        [pltpu.VMEM((cells // 128, 128), jnp.int32)],
+        4 << 30,
+        (starts, mask, snapshots),
+    )
+    got, blocks = lax.optimization_barrier((got, blocks))
+    mine = add(add(mine, got[0]), add(got[1], got[2]))
+    bit = 8
+    while bit < n:
+        mine = add(mine, other(mine, bit, n))
+        bit *= 2
+    counts = mine[0, size, :n].astype(jnp.int32)
+    quarters = gather_quarters(mine[:, :size], n)
+    outgoing = call(
+        functools.partial(turn_kernel, n),
+        "turn",
+        jax.ShapeDtypeStruct((n, slots, k), F32),
+        [SMEM, SMEM, VMEM],
+        [pltpu.SemaphoreType.DMA((n,))],
+        1 << 20,
+        (own_list, counts, blocks),
+        out_space=HBM,
+    )
+    quarters, outgoing = lax.optimization_barrier((quarters, outgoing))
     received = lax.all_to_all(outgoing, "height", split_axis=0, concat_axis=0, tiled=True)
-    pair = reduce_pair(pair, n, own)
+    half = assemble(quarters, own)
+    got = other(half, 1, n)
     square = jax.ShapeDtypeStruct((k, k), F32)
     inverse, factor = call(
         chain_kernel,
         "chain",
         [square, square],
-        [VMEM],
+        [SMEM, VMEM, VMEM],
         [pltpu.VMEM((k, k), F32)] * 4,
         20 << 30,
-        (pair,),
+        (own_list, half, got),
     )
     modes = call(
         functools.partial(modes_kernel, n, slots),
         "modes",
         jax.ShapeDtypeStruct((BLK, k), F32),
         [SMEM, SMEM, VMEM, VMEM],
-        [pltpu.VMEM((BLK + slots + 8, k), F32)],
+        [pltpu.VMEM((BLK + slots + 8, k), F32), pltpu.VMEM((BLK, k), F32), pltpu.SemaphoreType.DMA((4,))],
         12 * BLK * k * k,
         (own_list, counts, received, inverse),
+        out_space=HBM,
     )
     return (modes, factor)
 

time: 88.5 us -> 73.4 us (0.83)
  Pallas kernels: 39.4 us -> 30.3 us
  waiting for transfers between devices: 27.4 us -> 19.2 us
  starting transfers between devices: 15.5 us -> 20 us
  other arithmetic: 2.82 us -> 0.57 us
    pallas_call x4 -> x6, Pallas kernels: 39.4 us -> 30.3 us  [call(): pl.pallas_call(kernel, name=name, out_shape=out, in_specs=in_specs, out_s...]
    ppermute x10 -> x9, waiting for transfers between devices: 11.6 us -> 3.4 us  [other(): return lax.ppermute(x, 'height', [(i, i ^ bits) for i in range(n)])]
    ppermute x10 -> x9, starting transfers between devices: 5.76 us -> 8.96 us  [other(): return lax.ppermute(x, 'height', [(i, i ^ bits) for i in range(n)])]
    add x8 -> x2, other arithmetic: 1.4 us -> 0.05 us  [add_pair(): return (total, a[1] + b[1] + error)]
    all_to_all x1, starting transfers between devices: 9.76 us -> 11 us  [local(): lax.all_to_all(outgoing, 'height', split_axis=0, concat_axis=0, tiled=True)]
  transfers between devices with their start and end apart: 11 -> 10, of which waited for: 7 -> 5; matrix products, arithmetic and copies ran while one was open for 3% -> 1% of each run, Pallas kernels for 37% -> 32%
where the time goes in v2:
time: 73.4 us; the launch traced here: 73.2 us
  Pallas kernels  30.3 us (41%)
  starting transfers between devices  20 us (27%)
  waiting for transfers between devices  19.2 us (26%)
  local copies, waits for them, and re-layouts  2.29 us (3%)
  between operations  0.91 us (1%)
    pallas_call x6, Pallas kernels, call(): pl.pallas_call(kernel, name=name, out_shape=out, in_specs=in_specs, out_s...  30.3 us
    all_to_all x1, waiting for transfers between devices, local(): lax.all_to_all(outgoing, 'height', split_axis=0, concat_axis=0, tiled=True)  15.8 us
    all_to_all x1, starting transfers between devices, local(): lax.all_to_all(outgoing, 'height', split_axis=0, concat_axis=0, tiled=True)  11 us
    ppermute x9, starting transfers between devices, other(): return lax.ppermute(x, 'height', [(i, i ^ bits) for i in range(n)])  8.96 us
    ppermute x9, waiting for transfers between devices, other(): return lax.ppermute(x, 'height', [(i, i ^ bits) for i in range(n)])  3.4 us
    unnamed x8, local copies, waits for them, and re-layouts  2.29 us
  transfers between devices with their start and end apart: 10, of which 5 were waited for; matrix products, arithmetic and copies ran while one was open for 1% of the time, Pallas kernels for 32%

profile of v2, /device:TPU:13, one launch (start us, length us, event | category | flops | bytes accessed | tf_op | source)
XLA Modules:
  0.0 73.2 jit_solution(15241097835719033243)
XLA Ops:
  0.6 0.0 copy-start
  0.6 0.7 copy-done
  1.3 0.0 copy-start.2
  1.3 1.6 %copy-done.2 = f32[2048,256]{1,0:T(8,128)S(1)} copy-done((f32[2048,256]{1,0:T(8,128)S(1)}, f32[2048,256]{1,0:T(8,128)}, u32[]{:S(2)}) %copy-start.2) | copy-done | bytes 2097176
  2.9 0.0 copy-start.1
  2.9 0.0 copy-start.3
  2.9 3.8 %gram.1 = (f32[2,200,128]{2,1,0:T(8,128)S(1)}, f32[2,200,128]{2,1,0:T(8,128)S(1)}) custom-call(s32[1]{0:T(128)} %bitcast.own_ref, f32[2048,256]{1,0:T(8,128)S(1)} %copy-done.2, s32[16,128]{1,0:T(8,128)S(1)} %bitcast.4), custom_call_target="tpu_custom_call" | custom-call | flops 2147483648 | bytes 4194304 | tf_op jit(solution)/shard_map/gram/pallas_call | solution.py:309
  6.7 0.7 collective-permute-start
  7.4 0.5 select_reduce_fusion.starts_ref
  7.9 0.6 collective-permute-done.got_ref
  8.6 0.1 collective-permute-start.1
  8.6 1.4 %collective-permute-start.2 = (f32[2,56,128]{2,1,0:T(8,128)S(1)}, f32[2,56,128]{2,1,0:T(8,128)S(1)}, u32[]{:S(2)}, u32[]{:S(2)}) collective-permute-start(f32[2,56,128]{2,1,0:T(8,128)S(1)} %get-tuple-element.26), channel_id=1, source_target_pairs={{0,4},{1,5},{2,6},{3,7},{4,0},{5,1},{6,2},{7,3},{8,12},{9,13},{10,... | collective-permute-start | bytes 172040 | tf_op jit(solution)/shard_map/ppermute | solution.py:322
  10.0 1.2 %collective-permute-start.3 = (f32[2,56,128]{2,1,0:T(8,128)S(1)}, f32[2,56,128]{2,1,0:T(8,128)S(1)}, u32[]{:S(2)}, u32[]{:S(2)}) collective-permute-start(f32[2,56,128]{2,1,0:T(8,128)S(1)} %get-tuple-element.27), channel_id=1, source_target_pairs={{0,2},{1,3},{2,0},{3,1},{4,6},{5,7},{6,4},{7,5},{8,10},{9,11},{10,... | collective-permute-start | bytes 172040 | tf_op jit(solution)/shard_map/ppermute | solution.py:322
  11.3 0.0 copy-done.1
  11.3 0.0 copy-done.3
  11.3 2.7 %compact.1.blocks_ref = f32[16,96,256]{2,1,0:T(8,128)S(1)} custom-call(s32[16]{0:T(128)S(1)} %select_reduce_fusion.starts_ref, s32[16,128]{1,0:T(8,128)S(1)} %bitcast.6, f32[2048,256]{1,0:T(8,128)S(1)} %copy-done.3), custom_call_target="tpu_custom_call" | custom-call | flops 4294967296 | bytes 4194304 | tf_op jit(solution)/shard_map/compact/pallas_call | solution.py:309
  14.0 0.0 collective-permute-done.1
  14.0 0.0 collective-permute-done.2
  14.0 0.0 collective-permute-done.3
  14.1 2.4 %collective-permute-start.4 = (f32[2,56,128]{2,1,0:T(8,128)S(1)}, f32[2,56,128]{2,1,0:T(8,128)S(1)}, u32[]{:S(2)}, u32[]{:S(2)}) collective-permute-start(f32[2,56,128]{2,1,0:T(8,128)S(1)} %pad_maximum_fusion.1), channel_id=1, source_target_pairs={{0,8},{1,9},{2,10},{3,11},{4,12},{5,13},{6,14},{7,15},{8,0},{9,1},... | collective-permute-start | bytes 172040 | tf_op jit(solution)/shard_map/ppermute | solution.py:322
  16.5 1.6 %collective-permute-done.4 = f32[2,56,128]{2,1,0:T(8,128)S(1)} collective-permute-done((f32[2,56,128]{2,1,0:T(8,128)S(1)}, f32[2,56,128]{2,1,0:T(8,128)S(1)}, u32[]{:S(2)}, u32[]{:S(2)}) %collective-permute-start.4) | collective-permute-done | bytes 57376 | tf_op jit(solution)/shard_map/ppermute | solution.py:322
  18.1 0.8 %collective-permute-start.5 = (f32[2,48,128]{2,1,0:T(8,128)S(1)}, f32[2,48,128]{2,1,0:T(8,128)S(1)}, u32[]{:S(2)}, u32[]{:S(2)}) collective-permute-start(f32[2,48,128]{2,1,0:T(8,128)S(1)} %pad_maximum_fusion.2), channel_id=1, source_target_pairs={{0,2},{1,3},{2,0},{3,1},{4,6},{5,7},{6,4},{7,5},{8,10},{9,11},{10,... | collective-permute-start | bytes 147464 | tf_op jit(solution)/shard_map/ppermute | solution.py:322
  19.0 0.0 collective-permute-start.6
  19.0 1.9 %collective-permute-start.7 = (f32[2,48,128]{2,1,0:T(8,128)S(1)}, f32[2,48,128]{2,1,0:T(8,128)S(1)}, u32[]{:S(2)}, u32[]{:S(2)}) collective-permute-start(f32[2,48,128]{2,1,0:T(8,128)S(1)} %pad_maximum_fusion.2), channel_id=1, source_target_pairs={{0,6},{1,7},{2,4},{3,5},{4,2},{5,3},{6,0},{7,1},{8,14},{9,15},{10,... | collective-permute-start | bytes 147464 | tf_op jit(solution)/shard_map/ppermute | solution.py:322
  20.9 1.9 %turn.1 = f32[16,96,256]{2,1,0:T(8,128)} custom-call(s32[1]{0:T(128)} %bitcast.own_ref, s32[16]{0:T(128)S(1)} %fusion.2.counts_ref, f32[16,96,256]{2,1,0:T(8,128)S(1)} %compact.1.blocks_ref), custom_call_target="tpu_custom_call" | custom-call | flops 1048576 | bytes 4194304 | tf_op jit(solution)/shard_map/turn/pallas_call | solution.py:309
  22.8 0.0 collective-permute-done.5
  22.8 0.0 collective-permute-done.6
  22.8 0.1 collective-permute-done.7
  22.9 11.0 %all-to-all-start = ((f32[16,96,256]{2,1,0:T(8,128)}), f32[16,96,256]{2,1,0:T(8,128)S(1)}, u32[]{:S(2)}, u32[]{:S(2)}) async-start(f32[16,96,256]{2,1,0:T(8,128)} %turn.1), calls=%async_computation | async-start | bytes 3145728 | tf_op jit(solution)/shard_map/all_to_all | solution.py:398
  33.9 0.4 collective-permute-start.8
  34.3 1.1 %collective-permute-done.8.got_ref = f32[2,192,128]{2,1,0:T(8,128)S(1)} collective-permute-done((f32[2,192,128]{2,1,0:T(8,128)S(1)}, f32[2,192,128]{2,1,0:T(8,128)S(1)}, u32[]{:S(2)}, u32[]{:S(2)}) %collective-permute-start.8) | collective-permute-done | bytes 196640 | tf_op jit(solution)/shard_map/ppermute | solution.py:322
  35.4 18.9 %chain.1 = (f32[256,256]{1,0:T(8,128)S(1)}, f32[256,256]{1,0:T(8,128)}) custom-call(s32[1]{0:T(128)} %bitcast.own_ref, f32[2,192,128]{2,1,0:T(8,128)S(1)} %pad_maximum_fusion.half_ref, f32[2,192,128]{2,1,0:T(8,128)S(1)} %collective-permute-done.8.got_ref), custom_call_target="tpu_custom_call" | custom-call | flops 21474836480 | bytes 4194304 | tf_op jit(solution)/shard_map/chain/pallas_call | solution.py:309
  54.3 15.8 %all-to-all-done.recv_ref = f32[16,96,256]{2,1,0:T(8,128)S(1)} async-done(((f32[16,96,256]{2,1,0:T(8,128)}), f32[16,96,256]{2,1,0:T(8,128)S(1)}, u32[]{:S(2)}, u32[]{:S(2)}) %all-to-all-start) | async-done | bytes 1572896 | tf_op jit(solution)/shard_map/all_to_all | solution.py:398
  70.1 3.0 %modes.1 = f32[1024,256]{1,0:T(8,128)} custom-call(s32[1]{0:T(128)} %bitcast.own_ref, s32[16]{0:T(128)S(1)} %fusion.2.counts_ref, f32[16,96,256]{2,1,0:T(8,128)S(1)} %all-to-all-done.recv_ref, f32[256,256]{1,0:T(8,128)S(1)} %get-tuple-element.38.inv_ref), custom_call_target="tpu_custom_call" | custom-call | flops 805306368 | bytes 4194304 | tf_op jit(solution)/shard_map/modes/pallas_call | solution.py:309
  (9 shorter events, 0.1 us)
Async XLA Ops:
  0.6 0.7 copy-start
  1.3 1.6 %copy-start.2 = (f32[2048,256]{1,0:T(8,128)S(1)}, f32[2048,256]{1,0:T(8,128)}, u32[]{:S(2)}) copy-start(f32[2048,256]{1,0:T(8,128)} %x_ref.3) | copy-start | bytes 6291460
  2.9 8.3 %copy-start.1 = (s32[2048]{0:T(1024)S(1)}, s32[2048]{0:T(1024)}, u32[]{:S(2)}) copy-start(s32[2048]{0:T(1024)} %param.3) | copy-start | bytes 24580
  2.9 8.3 %copy-start.3 = (f32[2048,256]{1,0:T(8,128)S(1)}, f32[2048,256]{1,0:T(8,128)}, u32[]{:S(2)}) copy-start(f32[2048,256]{1,0:T(8,128)} %x_ref.3) | copy-start | bytes 6291460
  6.7 1.8 %collective-permute-start = (f32[2,200,128]{2,1,0:T(8,128)S(1)}, f32[2,200,128]{2,1,0:T(8,128)S(1)}, u32[]{:S(2)}, u32[]{:S(2)}) collective-permute-start(f32[2,200,128]{2,1,0:T(8,128)S(1)} %get-tuple-element.22), channel_id=1, source_target_pairs={{0,1},{1,0},{2,3},{3,2},{4,5},{5,4},{6,7},{7,6},{8,9},{9,8},{10,11... | collective-permute-start | bytes 614408 | tf_op jit(solution)/shard_map/ppermute | solution.py:322
  8.6 5.5 %collective-permute-start.1 = (f32[2,56,128]{2,1,0:T(8,128)S(1)}, f32[2,56,128]{2,1,0:T(8,128)S(1)}, u32[]{:S(2)}, u32[]{:S(2)}) collective-permute-start(f32[2,56,128]{2,1,0:T(8,128)S(1)} %get-tuple-element.25), channel_id=1, source_target_pairs={{0,6},{1,7},{2,4},{3,5},{4,2},{5,3},{6,0},{7,1},{8,14},{9,15},{10,... | collective-permute-start | bytes 172040 | tf_op jit(solution)/shard_map/ppermute | solution.py:322
  8.6 5.4 %collective-permute-start.2 = (f32[2,56,128]{2,1,0:T(8,128)S(1)}, f32[2,56,128]{2,1,0:T(8,128)S(1)}, u32[]{:S(2)}, u32[]{:S(2)}) collective-permute-start(f32[2,56,128]{2,1,0:T(8,128)S(1)} %get-tuple-element.26), channel_id=1, source_target_pairs={{0,4},{1,5},{2,6},{3,7},{4,0},{5,1},{6,2},{7,3},{8,12},{9,13},{10,... | collective-permute-start | bytes 172040 | tf_op jit(solution)/shard_map/ppermute | solution.py:322
  10.0 4.0 %collective-permute-start.3 = (f32[2,56,128]{2,1,0:T(8,128)S(1)}, f32[2,56,128]{2,1,0:T(8,128)S(1)}, u32[]{:S(2)}, u32[]{:S(2)}) collective-permute-start(f32[2,56,128]{2,1,0:T(8,128)S(1)} %get-tuple-element.27), channel_id=1, source_target_pairs={{0,2},{1,3},{2,0},{3,1},{4,6},{5,7},{6,4},{7,5},{8,10},{9,11},{10,... | collective-permute-start | bytes 172040 | tf_op jit(solution)/shard_map/ppermute | solution.py:322
  14.1 4.0 %collective-permute-start.4 = (f32[2,56,128]{2,1,0:T(8,128)S(1)}, f32[2,56,128]{2,1,0:T(8,128)S(1)}, u32[]{:S(2)}, u32[]{:S(2)}) collective-permute-start(f32[2,56,128]{2,1,0:T(8,128)S(1)} %pad_maximum_fusion.1), channel_id=1, source_target_pairs={{0,8},{1,9},{2,10},{3,11},{4,12},{5,13},{6,14},{7,15},{8,0},{9,1},... | collective-permute-start | bytes 172040 | tf_op jit(solution)/shard_map/ppermute | solution.py:322
  18.1 4.6 %collective-permute-start.5 = (f32[2,48,128]{2,1,0:T(8,128)S(1)}, f32[2,48,128]{2,1,0:T(8,128)S(1)}, u32[]{:S(2)}, u32[]{:S(2)}) collective-permute-start(f32[2,48,128]{2,1,0:T(8,128)S(1)} %pad_maximum_fusion.2), channel_id=1, source_target_pairs={{0,2},{1,3},{2,0},{3,1},{4,6},{5,7},{6,4},{7,5},{8,10},{9,11},{10,... | collective-permute-start | bytes 147464 | tf_op jit(solution)/shard_map/ppermute | solution.py:322
  19.0 3.8 %collective-permute-start.6 = (f32[2,48,128]{2,1,0:T(8,128)S(1)}, f32[2,48,128]{2,1,0:T(8,128)S(1)}, u32[]{:S(2)}, u32[]{:S(2)}) collective-permute-start(f32[2,48,128]{2,1,0:T(8,128)S(1)} %pad_maximum_fusion.2), channel_id=1, source_target_pairs={{0,4},{1,5},{2,6},{3,7},{4,0},{5,1},{6,2},{7,3},{8,12},{9,13},{10,... | collective-permute-start | bytes 147464 | tf_op jit(solution)/shard_map/ppermute | solution.py:322
  19.0 3.9 %collective-permute-start.7 = (f32[2,48,128]{2,1,0:T(8,128)S(1)}, f32[2,48,128]{2,1,0:T(8,128)S(1)}, u32[]{:S(2)}, u32[]{:S(2)}) collective-permute-start(f32[2,48,128]{2,1,0:T(8,128)S(1)} %pad_maximum_fusion.2), channel_id=1, source_target_pairs={{0,6},{1,7},{2,4},{3,5},{4,2},{5,3},{6,0},{7,1},{8,14},{9,15},{10,... | collective-permute-start | bytes 147464 | tf_op jit(solution)/shard_map/ppermute | solution.py:322
  22.9 47.2 %all-to-all-start = ((f32[16,96,256]{2,1,0:T(8,128)}), f32[16,96,256]{2,1,0:T(8,128)S(1)}, u32[]{:S(2)}, u32[]{:S(2)}) async-start(f32[16,96,256]{2,1,0:T(8,128)} %turn.1), calls=%async_computation | async-start | bytes 3145728 | tf_op jit(solution)/shard_map/all_to_all | solution.py:398
  33.9 1.5 %collective-permute-start.8 = (f32[2,192,128]{2,1,0:T(8,128)S(1)}, f32[2,192,128]{2,1,0:T(8,128)S(1)}, u32[]{:S(2)}, u32[]{:S(2)}) collective-permute-start(f32[2,192,128]{2,1,0:T(8,128)S(1)} %pad_maximum_fusion.half_ref), channel_id=1, source_target_pairs={{0,1},{1,0},{2,3},{3,2},{4,5},{5,4},{6,7},{7,6},{8,9},{9,8},{10,11... | collective-permute-start | bytes 589832 | tf_op jit(solution)/shard_map/ppermute | solution.py:322

commit v3 on v2

--- a/solution.py
+++ b/solution.py
@@ -263,7 +263,12 @@
 
 
 def turn_kernel(n, own_ref, counts_ref, blocks_ref, out_ref, sem):
-    start = lax.fori_loop(0, own_ref[0], lambda s, total: total + counts_ref[s], jnp.int32(0))
+    own = own_ref[0]
+    upper = own >= n // 2
+    add_count = lambda s, total: total + counts_ref[s]
+    low = jnp.where(upper, own, 0)
+    start = lax.fori_loop(low, jnp.where(upper, n, own), add_count, jnp.int32(0))
+    start = jnp.where(upper, -start, start)
     copies = [
         pltpu.make_async_copy(blocks_ref.at[(d - start) & (n - 1)], out_ref.at[d], sem.at[d]) for d in range(n)
     ]
@@ -327,7 +332,7 @@
 
 
 def gather_quarters(mine, n):
-    return [mine] + [other(mine, 2 * turn, n) for turn in (3, 2, 1)][::-1]
+    return [mine] + [other(mine, 2 * turn, n) for turn in (1, 2, 3)]
 
 
 def assemble(got, own):
@@ -380,6 +385,7 @@
     mine = add(add(mine, got[0]), add(got[1], got[2]))
     bit = 8
     while bit < n:
+        near_counts = mine[0, size, :n].astype(jnp.int32)
         mine = add(mine, other(mine, bit, n))
         bit *= 2
     counts = mine[0, size, :n].astype(jnp.int32)
@@ -391,10 +397,10 @@
         [SMEM, SMEM, VMEM],
         [pltpu.SemaphoreType.DMA((n,))],
         1 << 20,
-        (own_list, counts, blocks),
+        (own_list, near_counts, blocks),
         out_space=HBM,
     )
-    quarters, outgoing = lax.optimization_barrier((quarters, outgoing))
+    outgoing, counts = lax.optimization_barrier((outgoing, counts))
     received = lax.all_to_all(outgoing, "height", split_axis=0, concat_axis=0, tiled=True)
     half = assemble(quarters, own)
     got = other(half, 1, n)
@@ -405,7 +411,7 @@
         [square, square],
         [SMEM, VMEM, VMEM],
         [pltpu.VMEM((k, k), F32)] * 4,
-        20 << 30,
+        25 << 30,
         (own_list, half, got),
     )
     modes = call(

time: 73.4 us -> 70 us (0.954)
  starting transfers between devices: 20 us -> 18.2 us
  waiting for transfers between devices: 19.2 us -> 17.4 us
    all_to_all x1, starting transfers between devices: 11 us -> 9.26 us  [local(): lax.all_to_all(outgoing, 'height', split_axis=0, concat_axis=0, tiled=True)]
    ppermute x9, waiting for transfers between devices: 3.4 us -> 1.71 us  [other(): return lax.ppermute(x, 'height', [(i, i ^ bits) for i in range(n)])]
  transfers between devices with their start and end apart: 10 -> 10, of which waited for: 5 -> 3; matrix products, arithmetic and copies ran while one was open for 1% -> 1% of each run, Pallas kernels for 32% -> 34%
where the time goes in v3:
time: 70 us; the launch traced here: 69.7 us
  Pallas kernels  30.3 us (43%)
  starting transfers between devices  18.2 us (26%)
  waiting for transfers between devices  17.4 us (25%)
  local copies, waits for them, and re-layouts  2.29 us (3%)
  between operations  0.93 us (1%)
    pallas_call x6, Pallas kernels, call(): pl.pallas_call(kernel, name=name, out_shape=out, in_specs=in_specs, out_s...  30.3 us
    all_to_all x1, waiting for transfers between devices, local(): lax.all_to_all(outgoing, 'height', split_axis=0, concat_axis=0, tiled=True)  15.7 us
    all_to_all x1, starting transfers between devices, local(): lax.all_to_all(outgoing, 'height', split_axis=0, concat_axis=0, tiled=True)  9.26 us
    ppermute x9, starting transfers between devices, other(): return lax.ppermute(x, 'height', [(i, i ^ bits) for i in range(n)])  8.97 us
    unnamed x8, local copies, waits for them, and re-layouts  2.29 us
    ppermute x9, waiting for transfers between devices, other(): return lax.ppermute(x, 'height', [(i, i ^ bits) for i in range(n)])  1.71 us
  transfers between devices with their start and end apart: 10, of which 3 were waited for; matrix products, arithmetic and copies ran while one was open for 1% of the time, Pallas kernels for 34%

profile of v3, /device:TPU:13, one launch (start us, length us, event | category | flops | bytes accessed | tf_op | source)
XLA Modules:
  0.0 69.7 jit_solution(14903707417359969272)
XLA Ops:
  0.6 0.0 copy-start
  0.6 0.7 copy-done
  1.3 0.0 copy-start.2
  1.3 1.6 %copy-done.2 = f32[2048,256]{1,0:T(8,128)S(1)} copy-done((f32[2048,256]{1,0:T(8,128)S(1)}, f32[2048,256]{1,0:T(8,128)}, u32[]{:S(2)}) %copy-start.2) | copy-done | bytes 2097176
  2.9 0.0 copy-start.1
  2.9 0.0 copy-start.3
  2.9 3.8 %gram.1 = (f32[2,200,128]{2,1,0:T(8,128)S(1)}, f32[2,200,128]{2,1,0:T(8,128)S(1)}) custom-call(s32[1]{0:T(128)} %bitcast.own_ref, f32[2048,256]{1,0:T(8,128)S(1)} %copy-done.2, s32[16,128]{1,0:T(8,128)S(1)} %bitcast.6), custom_call_target="tpu_custom_call" | custom-call | flops 2147483648 | bytes 4194304 | tf_op jit(solution)/shard_map/gram/pallas_call | solution.py:314
  6.7 0.7 %collective-permute-start = (f32[2,200,128]{2,1,0:T(8,128)S(1)}, f32[2,200,128]{2,1,0:T(8,128)S(1)}, u32[]{:S(2)}, u32[]{:S(2)}) collective-permute-start(f32[2,200,128]{2,1,0:T(8,128)S(1)} %get-tuple-element.19), channel_id=1, source_target_pairs={{0,1},{1,0},{2,3},{3,2},{4,5},{5,4},{6,7},{7,6},{8,9},{9,8},{10,11... | collective-permute-start | bytes 614408 | tf_op jit(solution)/shard_map/ppermute | solution.py:327
  7.4 0.0 copy-done.1
  7.4 0.5 select_reduce_fusion.starts_ref
  7.9 0.6 collective-permute-done.got_ref
  8.6 0.1 collective-permute-start.1
  8.6 1.4 %collective-permute-start.2 = (f32[2,56,128]{2,1,0:T(8,128)S(1)}, f32[2,56,128]{2,1,0:T(8,128)S(1)}, u32[]{:S(2)}, u32[]{:S(2)}) collective-permute-start(f32[2,56,128]{2,1,0:T(8,128)S(1)} %get-tuple-element.23), channel_id=1, source_target_pairs={{0,4},{1,5},{2,6},{3,7},{4,0},{5,1},{6,2},{7,3},{8,12},{9,13},{10,... | collective-permute-start | bytes 172040 | tf_op jit(solution)/shard_map/ppermute | solution.py:327
  10.0 1.2 %collective-permute-start.3 = (f32[2,56,128]{2,1,0:T(8,128)S(1)}, f32[2,56,128]{2,1,0:T(8,128)S(1)}, u32[]{:S(2)}, u32[]{:S(2)}) collective-permute-start(f32[2,56,128]{2,1,0:T(8,128)S(1)} %get-tuple-element.24), channel_id=1, source_target_pairs={{0,2},{1,3},{2,0},{3,1},{4,6},{5,7},{6,4},{7,5},{8,10},{9,11},{10,... | collective-permute-start | bytes 172040 | tf_op jit(solution)/shard_map/ppermute | solution.py:327
  11.3 0.0 copy-done.3
  11.3 2.7 %compact.1.blocks_ref = f32[16,96,256]{2,1,0:T(8,128)S(1)} custom-call(s32[16]{0:T(128)S(1)} %select_reduce_fusion.starts_ref, s32[16,128]{1,0:T(8,128)S(1)} %bitcast.8, f32[2048,256]{1,0:T(8,128)S(1)} %copy-done.3), custom_call_target="tpu_custom_call" | custom-call | flops 4294967296 | bytes 4194304 | tf_op jit(solution)/shard_map/compact/pallas_call | solution.py:314
  14.0 0.0 collective-permute-done.1
  14.0 0.0 collective-permute-done.2
  14.0 0.0 collective-permute-done.3
  14.1 2.4 %collective-permute-start.4 = (f32[2,56,128]{2,1,0:T(8,128)S(1)}, f32[2,56,128]{2,1,0:T(8,128)S(1)}, u32[]{:S(2)}, u32[]{:S(2)}) collective-permute-start(f32[2,56,128]{2,1,0:T(8,128)S(1)} %pad_maximum_fusion.1), channel_id=1, source_target_pairs={{0,8},{1,9},{2,10},{3,11},{4,12},{5,13},{6,14},{7,15},{8,0},{9,1},... | collective-permute-start | bytes 172040 | tf_op jit(solution)/shard_map/ppermute | solution.py:327
  16.5 1.9 %turn.1 = f32[16,96,256]{2,1,0:T(8,128)} custom-call(s32[1]{0:T(128)} %bitcast.own_ref, s32[16]{0:T(128)S(1)} %fusion.3.counts_ref, f32[16,96,256]{2,1,0:T(8,128)S(1)} %compact.1.blocks_ref), custom_call_target="tpu_custom_call" | custom-call | flops 1048576 | bytes 4194304 | tf_op jit(solution)/shard_map/turn/pallas_call | solution.py:314
  18.4 0.0 collective-permute-done.4
  18.4 0.8 %collective-permute-start.5 = (f32[2,48,128]{2,1,0:T(8,128)S(1)}, f32[2,48,128]{2,1,0:T(8,128)S(1)}, u32[]{:S(2)}, u32[]{:S(2)}) collective-permute-start(f32[2,48,128]{2,1,0:T(8,128)S(1)} %pad_maximum_fusion.2), channel_id=1, source_target_pairs={{0,2},{1,3},{2,0},{3,1},{4,6},{5,7},{6,4},{7,5},{8,10},{9,11},{10,... | collective-permute-start | bytes 147464 | tf_op jit(solution)/shard_map/ppermute | solution.py:327
  19.3 0.6 collective-permute-start.6
  19.8 1.3 %collective-permute-start.7 = (f32[2,48,128]{2,1,0:T(8,128)S(1)}, f32[2,48,128]{2,1,0:T(8,128)S(1)}, u32[]{:S(2)}, u32[]{:S(2)}) collective-permute-start(f32[2,48,128]{2,1,0:T(8,128)S(1)} %pad_maximum_fusion.2), channel_id=1, source_target_pairs={{0,4},{1,5},{2,6},{3,7},{4,0},{5,1},{6,2},{7,3},{8,12},{9,13},{10,... | collective-permute-start | bytes 147464 | tf_op jit(solution)/shard_map/ppermute | solution.py:327
  21.2 9.3 %all-to-all-start = ((f32[16,96,256]{2,1,0:T(8,128)}), f32[16,96,256]{2,1,0:T(8,128)S(1)}, u32[]{:S(2)}, u32[]{:S(2)}) async-start(f32[16,96,256]{2,1,0:T(8,128)} %turn.1), calls=%async_computation | async-start | bytes 3145728 | tf_op jit(solution)/shard_map/all_to_all | solution.py:404
  30.4 0.0 collective-permute-done.5
  30.4 0.0 collective-permute-done.6
  30.4 0.0 collective-permute-done.7
  30.5 0.4 collective-permute-start.8
  30.9 1.1 %collective-permute-done.8.got_ref = f32[2,192,128]{2,1,0:T(8,128)S(1)} collective-permute-done((f32[2,192,128]{2,1,0:T(8,128)S(1)}, f32[2,192,128]{2,1,0:T(8,128)S(1)}, u32[]{:S(2)}, u32[]{:S(2)}) %collective-permute-start.8) | collective-permute-done | bytes 196640 | tf_op jit(solution)/shard_map/ppermute | solution.py:327
  32.0 18.9 %chain.1 = (f32[256,256]{1,0:T(8,128)S(1)}, f32[256,256]{1,0:T(8,128)}) custom-call(s32[1]{0:T(128)} %bitcast.own_ref, f32[2,192,128]{2,1,0:T(8,128)S(1)} %pad_maximum_fusion.half_ref, f32[2,192,128]{2,1,0:T(8,128)S(1)} %collective-permute-done.8.got_ref), custom_call_target="tpu_custom_call" | custom-call | flops 26843545600 | bytes 4194304 | tf_op jit(solution)/shard_map/chain/pallas_call | solution.py:314
  50.9 15.7 %all-to-all-done.recv_ref = f32[16,96,256]{2,1,0:T(8,128)S(1)} async-done(((f32[16,96,256]{2,1,0:T(8,128)}), f32[16,96,256]{2,1,0:T(8,128)S(1)}, u32[]{:S(2)}, u32[]{:S(2)}) %all-to-all-start) | async-done | bytes 1572896 | tf_op jit(solution)/shard_map/all_to_all | solution.py:404
  66.6 3.0 %modes.1 = f32[1024,256]{1,0:T(8,128)} custom-call(s32[1]{0:T(128)} %bitcast.own_ref, s32[16]{0:T(128)S(1)} %fusion.2.counts_ref, f32[16,96,256]{2,1,0:T(8,128)S(1)} %all-to-all-done.recv_ref, f32[256,256]{1,0:T(8,128)S(1)} %get-tuple-element.32.inv_ref), custom_call_target="tpu_custom_call" | custom-call | flops 805306368 | bytes 4194304 | tf_op jit(solution)/shard_map/modes/pallas_call | solution.py:314
  (10 shorter events, 0.2 us)
Async XLA Ops:
  0.6 0.7 %copy-start = (s32[2048]{0:T(1024)S(1)}, s32[2048]{0:T(1024)}, u32[]{:S(2)}) copy-start(s32[2048]{0:T(1024)} %param.3) | copy-start | bytes 24580
  1.3 1.6 %copy-start.2 = (f32[2048,256]{1,0:T(8,128)S(1)}, f32[2048,256]{1,0:T(8,128)}, u32[]{:S(2)}) copy-start(f32[2048,256]{1,0:T(8,128)} %x_ref.3) | copy-start | bytes 6291460
  2.9 4.5 %copy-start.1 = (s32[2048]{0:T(1024)S(1)}, s32[2048]{0:T(1024)}, u32[]{:S(2)}) copy-start(s32[2048]{0:T(1024)} %param.3) | copy-start | bytes 24580
  2.9 8.3 %copy-start.3 = (f32[2048,256]{1,0:T(8,128)S(1)}, f32[2048,256]{1,0:T(8,128)}, u32[]{:S(2)}) copy-start(f32[2048,256]{1,0:T(8,128)} %x_ref.3) | copy-start | bytes 6291460
  6.7 1.8 %collective-permute-start = (f32[2,200,128]{2,1,0:T(8,128)S(1)}, f32[2,200,128]{2,1,0:T(8,128)S(1)}, u32[]{:S(2)}, u32[]{:S(2)}) collective-permute-start(f32[2,200,128]{2,1,0:T(8,128)S(1)} %get-tuple-element.19), channel_id=1, source_target_pairs={{0,1},{1,0},{2,3},{3,2},{4,5},{5,4},{6,7},{7,6},{8,9},{9,8},{10,11... | collective-permute-start | bytes 614408 | tf_op jit(solution)/shard_map/ppermute | solution.py:327
  8.6 5.5 %collective-permute-start.1 = (f32[2,56,128]{2,1,0:T(8,128)S(1)}, f32[2,56,128]{2,1,0:T(8,128)S(1)}, u32[]{:S(2)}, u32[]{:S(2)}) collective-permute-start(f32[2,56,128]{2,1,0:T(8,128)S(1)} %get-tuple-element.22), channel_id=1, source_target_pairs={{0,6},{1,7},{2,4},{3,5},{4,2},{5,3},{6,0},{7,1},{8,14},{9,15},{10,... | collective-permute-start | bytes 172040 | tf_op jit(solution)/shard_map/ppermute | solution.py:327
  8.6 5.4 %collective-permute-start.2 = (f32[2,56,128]{2,1,0:T(8,128)S(1)}, f32[2,56,128]{2,1,0:T(8,128)S(1)}, u32[]{:S(2)}, u32[]{:S(2)}) collective-permute-start(f32[2,56,128]{2,1,0:T(8,128)S(1)} %get-tuple-element.23), channel_id=1, source_target_pairs={{0,4},{1,5},{2,6},{3,7},{4,0},{5,1},{6,2},{7,3},{8,12},{9,13},{10,... | collective-permute-start | bytes 172040 | tf_op jit(solution)/shard_map/ppermute | solution.py:327
  10.0 4.0 %collective-permute-start.3 = (f32[2,56,128]{2,1,0:T(8,128)S(1)}, f32[2,56,128]{2,1,0:T(8,128)S(1)}, u32[]{:S(2)}, u32[]{:S(2)}) collective-permute-start(f32[2,56,128]{2,1,0:T(8,128)S(1)} %get-tuple-element.24), channel_id=1, source_target_pairs={{0,2},{1,3},{2,0},{3,1},{4,6},{5,7},{6,4},{7,5},{8,10},{9,11},{10,... | collective-permute-start | bytes 172040 | tf_op jit(solution)/shard_map/ppermute | solution.py:327
  14.1 4.3 %collective-permute-start.4 = (f32[2,56,128]{2,1,0:T(8,128)S(1)}, f32[2,56,128]{2,1,0:T(8,128)S(1)}, u32[]{:S(2)}, u32[]{:S(2)}) collective-permute-start(f32[2,56,128]{2,1,0:T(8,128)S(1)} %pad_maximum_fusion.1), channel_id=1, source_target_pairs={{0,8},{1,9},{2,10},{3,11},{4,12},{5,13},{6,14},{7,15},{8,0},{9,1},... | collective-permute-start | bytes 172040 | tf_op jit(solution)/shard_map/ppermute | solution.py:327
  18.4 12.0 %collective-permute-start.5 = (f32[2,48,128]{2,1,0:T(8,128)S(1)}, f32[2,48,128]{2,1,0:T(8,128)S(1)}, u32[]{:S(2)}, u32[]{:S(2)}) collective-permute-start(f32[2,48,128]{2,1,0:T(8,128)S(1)} %pad_maximum_fusion.2), channel_id=1, source_target_pairs={{0,2},{1,3},{2,0},{3,1},{4,6},{5,7},{6,4},{7,5},{8,10},{9,11},{10,... | collective-permute-start | bytes 147464 | tf_op jit(solution)/shard_map/ppermute | solution.py:327
  19.3 11.2 %collective-permute-start.6 = (f32[2,48,128]{2,1,0:T(8,128)S(1)}, f32[2,48,128]{2,1,0:T(8,128)S(1)}, u32[]{:S(2)}, u32[]{:S(2)}) collective-permute-start(f32[2,48,128]{2,1,0:T(8,128)S(1)} %pad_maximum_fusion.2), channel_id=1, source_target_pairs={{0,6},{1,7},{2,4},{3,5},{4,2},{5,3},{6,0},{7,1},{8,14},{9,15},{10,... | collective-permute-start | bytes 147464 | tf_op jit(solution)/shard_map/ppermute | solution.py:327
  19.8 10.6 %collective-permute-start.7 = (f32[2,48,128]{2,1,0:T(8,128)S(1)}, f32[2,48,128]{2,1,0:T(8,128)S(1)}, u32[]{:S(2)}, u32[]{:S(2)}) collective-permute-start(f32[2,48,128]{2,1,0:T(8,128)S(1)} %pad_maximum_fusion.2), channel_id=1, source_target_pairs={{0,4},{1,5},{2,6},{3,7},{4,0},{5,1},{6,2},{7,3},{8,12},{9,13},{10,... | collective-permute-start | bytes 147464 | tf_op jit(solution)/shard_map/ppermute | solution.py:327
  21.2 45.4 %all-to-all-start = ((f32[16,96,256]{2,1,0:T(8,128)}), f32[16,96,256]{2,1,0:T(8,128)S(1)}, u32[]{:S(2)}, u32[]{:S(2)}) async-start(f32[16,96,256]{2,1,0:T(8,128)} %turn.1), calls=%async_computation | async-start | bytes 3145728 | tf_op jit(solution)/shard_map/all_to_all | solution.py:404
  30.5 1.5 %collective-permute-start.8 = (f32[2,192,128]{2,1,0:T(8,128)S(1)}, f32[2,192,128]{2,1,0:T(8,128)S(1)}, u32[]{:S(2)}, u32[]{:S(2)}) collective-permute-start(f32[2,192,128]{2,1,0:T(8,128)S(1)} %pad_maximum_fusion.half_ref), channel_id=1, source_target_pairs={{0,1},{1,0},{2,3},{3,2},{4,5},{5,4},{6,7},{7,6},{8,9},{9,8},{10,11... | collective-permute-start | bytes 589832 | tf_op jit(solution)/shard_map/ppermute | solution.py:327

commit v4 on v3

--- a/solution.py
+++ b/solution.py
@@ -176,42 +176,56 @@
     odd = (own_ref[0] & 1) > 0
     live = jnp.sum(mask_ref[...].astype(F32), axis=(0, 1), keepdims=True)
     lane = lax.broadcasted_iota(jnp.int32, (8, 128), 1)
-    count = jnp.where(lane == own_ref[0], live, 0.0)
+    row = lax.broadcasted_iota(jnp.int32, (8, 128), 0)
+    count = jnp.where((lane == own_ref[0]) & (row == 0), live, 0.0)
     for index, value in enumerate(pair):
         value = value * column * grow
-        blocks = (value[0:128, 0:128], value[0:128, 128:256], value[128:256, 128:256])
-        first = jnp.concatenate([blocks[0], blocks[1][0:64]], 0)
-        second = jnp.concatenate([blocks[1][64:128], blocks[2]], 0)
+        last = value[128:256, 128:256]
+        first = value[0:128, 128:256]
+        second = jnp.where(upper_half(), value[0:128, 0:128], last)
+        extra = jnp.sum(jnp.where(diagonal(), last, 0.0), axis=0, keepdims=True)
+        extra = jnp.where(row == 1, extra, count if index == 0 else 0.0)
         size = first.shape[0]
         keep_ref[index, 0:size] = jnp.where(odd, second, first)
         send_ref[index, 0:size] = jnp.where(odd, first, second)
         for ref in (keep_ref, send_ref):
-            ref[index, size:] = count if index == 0 else jnp.zeros_like(count)
-
-
-def quarter_kernel(own_ref, keep_ref, got_ref, mine_ref, *send_refs):
+            ref[index, size:] = extra
+
+
+def quarter_kernel(own_ref, keep_ref, got_ref, mine_ref, send_ref):
     size = mine_ref.shape[1] - 8
-    place = (own_ref[0] >> 1) & 3
-    for turn, ref in enumerate((mine_ref,) + send_refs):
+    place = (own_ref[0] >> 1) & 1
+    for turn, ref in enumerate((mine_ref, send_ref)):
         for to, at in (
             (pl.ds(0, size), pl.ds(pl.multiple_of((place ^ turn) * size, 8), size)),
-            (pl.ds(size, 8), pl.ds(4 * size, 8)),
+            (pl.ds(size, 8), pl.ds(2 * size, 8)),
         ):
             ref[0, to, :], ref[1, to, :] = add_pair(
                 (keep_ref[0, at, :], keep_ref[1, at, :]), (got_ref[0, at, :], got_ref[1, at, :])
             )
 
 
-def unpack(p):
-    a, b, d = p[0:128], p[128:256], p[256:384]
-    return jnp.concatenate([jnp.concatenate([a, b], 1), jnp.concatenate([b.T, d], 1)], 0)
-
-
-def chain_kernel(own_ref, half_ref, got_ref, inv_ref, factor_ref, r1, w1, r2, w2):
+def upper_half():
+    return lax.broadcasted_iota(jnp.int32, (128, 128), 0) <= lax.broadcasted_iota(jnp.int32, (128, 128), 1)
+
+
+def diagonal():
+    return lax.broadcasted_iota(jnp.int32, (128, 128), 0) == lax.broadcasted_iota(jnp.int32, (128, 128), 1)
+
+
+def unpack(right, mixed, extra):
+    upper = jnp.where(upper_half(), mixed, 0.0)
+    lower = mixed - upper
+    first = upper + jnp.where(diagonal(), 0.0, upper).T
+    last = lower + lower.T + jnp.where(diagonal(), extra, 0.0)
+    return jnp.concatenate([jnp.concatenate([first, right], 1), jnp.concatenate([right.T, last], 1)], 0)
+
+
+def chain_kernel(own_ref, half_ref, got_ref, extra_ref, inv_ref, factor_ref, r1, w1, r2, w2):
     odd = (own_ref[0] & 1) > 0
     hi, lo = (
-        unpack(jnp.concatenate([jnp.where(odd, got, half), jnp.where(odd, half, got)], 0))
-        for half, got in ((half_ref[0], got_ref[0]), (half_ref[1], got_ref[1]))
+        unpack(jnp.where(odd, got_ref[i], half_ref[i]), jnp.where(odd, half_ref[i], got_ref[i]), extra_ref[i, 1:2, :])
+        for i in range(2)
     )
     sweep(block_upper(hi), r1, w1)
     r = r1[...]
@@ -331,21 +345,6 @@
     return jnp.stack(add_pair(a, b))
 
 
-def gather_quarters(mine, n):
-    return [mine] + [other(mine, 2 * turn, n) for turn in (1, 2, 3)]
-
-
-def assemble(got, own):
-    place = (own >> 1) & 3
-    return jnp.concatenate(
-        [
-            jnp.where(place < 2, *(jnp.where((place & 1) > 0, got[c ^ h ^ 1], got[c ^ h]) for h in (0, 2)))
-            for c in range(4)
-        ],
-        1,
-    )
-
-
 def local(snapshots, fluid_mask):
     n = lax.axis_size("height")
     own = lax.axis_index("height")
@@ -355,7 +354,7 @@
     mask = fluid_mask.reshape(cells // 128, 128)
     block = jnp.arange(cells // 128)
     starts = jnp.sum(jnp.where(block[None, :, None] < block[:, None, None], mask[None], 0), (1, 2))
-    half = jax.ShapeDtypeStruct((2, 200, 128), F32)
+    half = jax.ShapeDtypeStruct((2, 136, 128), F32)
     keep, send = call(
         functools.partial(gram_kernel, 1.0 / (n * BLK)),
         "gram",
@@ -365,12 +364,12 @@
         16 * cells * k * k,
         (own_list, snapshots, mask),
     )
-    size = keep.shape[1] // 4 // 8 * 8
+    size = (keep.shape[1] - 8) // 2
     quarter = jax.ShapeDtypeStruct((2, size + 8, 128), F32)
-    mine, side, up, across = call(
-        quarter_kernel, "quarter", [quarter] * 4, [SMEM, VMEM, VMEM], [], 1 << 20, (own_list, keep, other(send, 1, n))
-    )
-    got = [other(across, 6, n), other(up, 4, n), other(side, 2, n)]
+    mine, sent = call(
+        quarter_kernel, "quarter", [quarter] * 2, [SMEM, VMEM, VMEM], [], 1 << 20, (own_list, keep, other(send, 1, n))
+    )
+    got = other(sent, 2, n)
     starts, mine = lax.optimization_barrier((starts, mine))
     blocks = call(
         functools.partial(compact_kernel, n),
@@ -382,14 +381,15 @@
         (starts, mask, snapshots),
     )
     got, blocks = lax.optimization_barrier((got, blocks))
-    mine = add(add(mine, got[0]), add(got[1], got[2]))
-    bit = 8
+    mine = add(mine, got)
+    bit = 4
     while bit < n:
         near_counts = mine[0, size, :n].astype(jnp.int32)
         mine = add(mine, other(mine, bit, n))
         bit *= 2
     counts = mine[0, size, :n].astype(jnp.int32)
-    quarters = gather_quarters(mine[:, :size], n)
+    extra = mine[:, size:]
+    mine = mine[:, :size]
     outgoing = call(
         functools.partial(turn_kernel, n),
         "turn",
@@ -400,19 +400,20 @@
         (own_list, near_counts, blocks),
         out_space=HBM,
     )
-    outgoing, counts = lax.optimization_barrier((outgoing, counts))
     received = lax.all_to_all(outgoing, "height", split_axis=0, concat_axis=0, tiled=True)
-    half = assemble(quarters, own)
+    got = other(mine, 2, n)
+    high = (own & 2) > 0
+    half = jnp.concatenate([jnp.where(high, got, mine), jnp.where(high, mine, got)], 1)
     got = other(half, 1, n)
     square = jax.ShapeDtypeStruct((k, k), F32)
     inverse, factor = call(
         chain_kernel,
         "chain",
         [square, square],
-        [SMEM, VMEM, VMEM],
+        [SMEM, VMEM, VMEM, VMEM],
         [pltpu.VMEM((k, k), F32)] * 4,
-        25 << 30,
-        (own_list, half, got),
+        20 << 30,
+        (own_list, half, got, extra),
     )
     modes = call(
         functools.partial(modes_kernel, n, slots),

time: 70 us -> 65.8 us (0.940)
  starting transfers between devices: 18.2 us -> 11.7 us
  waiting for transfers between devices: 17.4 us -> 19.7 us
    ppermute x9 -> x6, waiting for transfers between devices: 1.71 us -> 13.4 us  [other(): return lax.ppermute(x, 'height', [(i, i ^ bits) for i in range(n)])]
    all_to_all x1, waiting for transfers between devices: 15.7 us -> 6.34 us  [local(): lax.all_to_all(outgoing, 'height', split_axis=0, concat_axis=0, tiled=True)]
    ppermute x9 -> x6, starting transfers between devices: 8.97 us -> 4.93 us  [other(): return lax.ppermute(x, 'height', [(i, i ^ bits) for i in range(n)])]
    all_to_all x1, starting transfers between devices: 9.26 us -> 6.8 us  [local(): lax.all_to_all(outgoing, 'height', split_axis=0, concat_axis=0, tiled=True)]
  transfers between devices with their start and end apart: 10 -> 7, of which waited for: 3 -> 6; matrix products, arithmetic and copies ran while one was open for 1% -> 1% of each run, Pallas kernels for 34% -> 36%
where the time goes in v4:
time: 65.8 us; the launch traced here: 65.5 us
  Pallas kernels  30.3 us (46%)
  waiting for transfers between devices  19.7 us (30%)
  starting transfers between devices  11.7 us (18%)
  local copies, waits for them, and re-layouts  2.29 us (3%)
  between operations  0.88 us (1%)
    pallas_call x6, Pallas kernels, call(): pl.pallas_call(kernel, name=name, out_shape=out, in_specs=in_specs, out_s...  30.3 us
    ppermute x6, waiting for transfers between devices, other(): return lax.ppermute(x, 'height', [(i, i ^ bits) for i in range(n)])  13.4 us
    all_to_all x1, starting transfers between devices, local(): lax.all_to_all(outgoing, 'height', split_axis=0, concat_axis=0, tiled=True)  6.8 us
    all_to_all x1, waiting for transfers between devices, local(): lax.all_to_all(outgoing, 'height', split_axis=0, concat_axis=0, tiled=True)  6.34 us
    ppermute x6, starting transfers between devices, other(): return lax.ppermute(x, 'height', [(i, i ^ bits) for i in range(n)])  4.93 us
    unnamed x8, local copies, waits for them, and re-layouts  2.29 us
  transfers between devices with their start and end apart: 7, of which 6 were waited for; matrix products, arithmetic and copies ran while one was open for 1% of the time, Pallas kernels for 36%

profile of v4, /device:TPU:13, one launch (start us, length us, event | category | flops | bytes accessed | tf_op | source)
XLA Modules:
  0.0 65.5 jit_solution(16567146559509991729)
XLA Ops:
  0.6 0.0 copy-start
  0.6 0.7 %copy-done = s32[2048]{0:T(1024)S(1)} copy-done((s32[2048]{0:T(1024)S(1)}, s32[2048]{0:T(1024)}, u32[]{:S(2)}) %copy-start) | copy-done | bytes 8216
  1.3 0.0 copy-start.2
  1.3 1.6 %copy-done.2 = f32[2048,256]{1,0:T(8,128)S(1)} copy-done((f32[2048,256]{1,0:T(8,128)S(1)}, f32[2048,256]{1,0:T(8,128)}, u32[]{:S(2)}) %copy-start.2) | copy-done | bytes 2097176
  2.9 0.0 copy-start.1
  2.9 0.0 copy-start.3
  2.9 3.8 %gram.1 = (f32[2,136,128]{2,1,0:T(8,128)S(1)}, f32[2,136,128]{2,1,0:T(8,128)S(1)}) custom-call(s32[1]{0:T(128)} %bitcast.own_ref, f32[2048,256]{1,0:T(8,128)S(1)} %copy-done.2, s32[16,128]{1,0:T(8,128)S(1)} %bitcast.6), custom_call_target="tpu_custom_call" | custom-call | flops 2147483648 | bytes 4194304 | tf_op jit(solution)/shard_map/gram/pallas_call | solution.py:328
  6.7 0.7 %collective-permute-start = (f32[2,136,128]{2,1,0:T(8,128)S(1)}, f32[2,136,128]{2,1,0:T(8,128)S(1)}, u32[]{:S(2)}, u32[]{:S(2)}) collective-permute-start(f32[2,136,128]{2,1,0:T(8,128)S(1)} %get-tuple-element.13), channel_id=1, source_target_pairs={{0,1},{1,0},{2,3},{3,2},{4,5},{5,4},{6,7},{7,6},{8,9},{9,8},{10,11... | collective-permute-start | bytes 417800 | tf_op jit(solution)/shard_map/ppermute | solution.py:341
  7.4 0.5 select_reduce_fusion.starts_ref
  7.9 0.5 collective-permute-done.got_ref
  8.5 0.3 collective-permute-start.1
  8.8 0.0 copy-done.1
  8.8 0.0 copy-done.3
  8.8 2.7 %compact.1.blocks_ref = f32[16,96,256]{2,1,0:T(8,128)S(1)} custom-call(s32[16]{0:T(128)S(1)} %select_reduce_fusion.starts_ref, s32[16,128]{1,0:T(8,128)S(1)} %bitcast.8, f32[2048,256]{1,0:T(8,128)S(1)} %copy-done.3), custom_call_target="tpu_custom_call" | custom-call | flops 4294967296 | bytes 4194304 | tf_op jit(solution)/shard_map/compact/pallas_call | solution.py:328
  11.5 0.2 collective-permute-done.1
  11.8 0.2 collective-permute-start.2
  12.0 3.0 %collective-permute-done.2 = f32[2,72,128]{2,1,0:T(8,128)S(1)} collective-permute-done((f32[2,72,128]{2,1,0:T(8,128)S(1)}, f32[2,72,128]{2,1,0:T(8,128)S(1)}, u32[]{:S(2)}, u32[]{:S(2)}) %collective-permute-start.2) | collective-permute-done | bytes 73760 | tf_op jit(solution)/shard_map/ppermute | solution.py:341
  15.1 2.4 %collective-permute-start.3 = (f32[2,72,128]{2,1,0:T(8,128)S(1)}, f32[2,72,128]{2,1,0:T(8,128)S(1)}, u32[]{:S(2)}, u32[]{:S(2)}) collective-permute-start(f32[2,72,128]{2,1,0:T(8,128)S(1)} %pad_maximum_fusion.2), channel_id=1, source_target_pairs={{0,8},{1,9},{2,10},{3,11},{4,12},{5,13},{6,14},{7,15},{8,0},{9,1},... | collective-permute-start | bytes 221192 | tf_op jit(solution)/shard_map/ppermute | solution.py:341
  17.4 1.9 %turn.1 = f32[16,96,256]{2,1,0:T(8,128)} custom-call(s32[1]{0:T(128)} %bitcast.own_ref, s32[16]{0:T(128)S(1)} %fusion.3.counts_ref, f32[16,96,256]{2,1,0:T(8,128)S(1)} %compact.1.blocks_ref), custom_call_target="tpu_custom_call" | custom-call | flops 1048576 | bytes 4194304 | tf_op jit(solution)/shard_map/turn/pallas_call | solution.py:328
  19.4 6.8 %all-to-all-start = ((f32[16,96,256]{2,1,0:T(8,128)}), f32[16,96,256]{2,1,0:T(8,128)S(1)}, u32[]{:S(2)}, u32[]{:S(2)}) async-start(f32[16,96,256]{2,1,0:T(8,128)} %turn.1), calls=%async_computation | async-start | bytes 3145728 | tf_op jit(solution)/shard_map/all_to_all | solution.py:403
  26.2 0.0 collective-permute-done.3
  26.2 0.3 collective-permute-start.4
  26.6 8.6 %collective-permute-done.4 = f32[2,64,128]{2,1,0:T(8,128)S(1)} collective-permute-done((f32[2,64,128]{2,1,0:T(8,128)S(1)}, f32[2,64,128]{2,1,0:T(8,128)S(1)}, u32[]{:S(2)}, u32[]{:S(2)}) %collective-permute-start.4) | collective-permute-done | bytes 65568 | tf_op jit(solution)/shard_map/ppermute | solution.py:341
  35.2 0.9 %collective-permute-start.5 = (f32[2,128,128]{2,1,0:T(8,128)S(1)}, f32[2,128,128]{2,1,0:T(8,128)S(1)}, u32[]{:S(2)}, u32[]{:S(2)}) collective-permute-start(f32[2,128,128]{2,1,0:T(8,128)S(1)} %pad_maximum_fusion.half_ref), channel_id=1, source_target_pairs={{0,1},{1,0},{2,3},{3,2},{4,5},{5,4},{6,7},{7,6},{8,9},{9,8},{10,11... | collective-permute-start | bytes 393224 | tf_op jit(solution)/shard_map/ppermute | solution.py:341
  36.1 1.0 %collective-permute-done.5.got_ref = f32[2,128,128]{2,1,0:T(8,128)S(1)} collective-permute-done((f32[2,128,128]{2,1,0:T(8,128)S(1)}, f32[2,128,128]{2,1,0:T(8,128)S(1)}, u32[]{:S(2)}, u32[]{:S(2)}) %collective-permute-start.5) | collective-permute-done | bytes 131104 | tf_op jit(solution)/shard_map/ppermute | solution.py:341
  37.1 18.9 %chain.1 = (f32[256,256]{1,0:T(8,128)S(1)}, f32[256,256]{1,0:T(8,128)}) custom-call(s32[1]{0:T(128)} %bitcast.own_ref, f32[2,128,128]{2,1,0:T(8,128)S(1)} %pad_maximum_fusion.half_ref, f32[2,128,128]{2,1,0:T(8,128)S(1)} %collective-permute-done.5.got_ref, f32[2,8,128]{2,1,0:T(8,128)S(1)} %pad_maximum_fusion.3.extra_ref), custom_call_target="tpu_custom_call" | custom-call | flops 21474836480 | bytes 4194304 | tf_op jit(solution)/shard_map/chain/pallas_call | solution.py:328
  56.1 6.3 %all-to-all-done.recv_ref = f32[16,96,256]{2,1,0:T(8,128)S(1)} async-done(((f32[16,96,256]{2,1,0:T(8,128)}), f32[16,96,256]{2,1,0:T(8,128)S(1)}, u32[]{:S(2)}, u32[]{:S(2)}) %all-to-all-start) | async-done | bytes 1572896 | tf_op jit(solution)/shard_map/all_to_all | solution.py:403
  62.4 3.0 %modes.1 = f32[1024,256]{1,0:T(8,128)} custom-call(s32[1]{0:T(128)} %bitcast.own_ref, s32[16]{0:T(128)S(1)} %fusion.4.counts_ref, f32[16,96,256]{2,1,0:T(8,128)S(1)} %all-to-all-done.recv_ref, f32[256,256]{1,0:T(8,128)S(1)} %get-tuple-element.20.inv_ref), custom_call_target="tpu_custom_call" | custom-call | flops 805306368 | bytes 4194304 | tf_op jit(solution)/shard_map/modes/pallas_call | solution.py:328
  (13 shorter events, 0.2 us)
Async XLA Ops:
  0.6 0.7 %copy-start = (s32[2048]{0:T(1024)S(1)}, s32[2048]{0:T(1024)}, u32[]{:S(2)}) copy-start(s32[2048]{0:T(1024)} %param.3) | copy-start | bytes 24580
  1.3 1.6 %copy-start.2 = (f32[2048,256]{1,0:T(8,128)S(1)}, f32[2048,256]{1,0:T(8,128)}, u32[]{:S(2)}) copy-start(f32[2048,256]{1,0:T(8,128)} %x_ref.3) | copy-start | bytes 6291460
  2.9 5.8 %copy-start.1 = (s32[2048]{0:T(1024)S(1)}, s32[2048]{0:T(1024)}, u32[]{:S(2)}) copy-start(s32[2048]{0:T(1024)} %param.3) | copy-start | bytes 24580
  2.9 5.8 %copy-start.3 = (f32[2048,256]{1,0:T(8,128)S(1)}, f32[2048,256]{1,0:T(8,128)}, u32[]{:S(2)}) copy-start(f32[2048,256]{1,0:T(8,128)} %x_ref.3) | copy-start | bytes 6291460
  6.7 1.7 %collective-permute-start = (f32[2,136,128]{2,1,0:T(8,128)S(1)}, f32[2,136,128]{2,1,0:T(8,128)S(1)}, u32[]{:S(2)}, u32[]{:S(2)}) collective-permute-start(f32[2,136,128]{2,1,0:T(8,128)S(1)} %get-tuple-element.13), channel_id=1, source_target_pairs={{0,1},{1,0},{2,3},{3,2},{4,5},{5,4},{6,7},{7,6},{8,9},{9,8},{10,11... | collective-permute-start | bytes 417800 | tf_op jit(solution)/shard_map/ppermute | solution.py:341
  8.5 3.3 %collective-permute-start.1 = (f32[2,72,128]{2,1,0:T(8,128)S(1)}, f32[2,72,128]{2,1,0:T(8,128)S(1)}, u32[]{:S(2)}, u32[]{:S(2)}) collective-permute-start(f32[2,72,128]{2,1,0:T(8,128)S(1)} %get-tuple-element.16), channel_id=1, source_target_pairs={{0,2},{1,3},{2,0},{3,1},{4,6},{5,7},{6,4},{7,5},{8,10},{9,11},{10,... | collective-permute-start | bytes 221192 | tf_op jit(solution)/shard_map/ppermute | solution.py:341
  11.8 3.3 %collective-permute-start.2 = (f32[2,72,128]{2,1,0:T(8,128)S(1)}, f32[2,72,128]{2,1,0:T(8,128)S(1)}, u32[]{:S(2)}, u32[]{:S(2)}) collective-permute-start(f32[2,72,128]{2,1,0:T(8,128)S(1)} %pad_maximum_fusion.1), channel_id=1, source_target_pairs={{0,4},{1,5},{2,6},{3,7},{4,0},{5,1},{6,2},{7,3},{8,12},{9,13},{10,... | collective-permute-start | bytes 221192 | tf_op jit(solution)/shard_map/ppermute | solution.py:341
  15.1 11.1 %collective-permute-start.3 = (f32[2,72,128]{2,1,0:T(8,128)S(1)}, f32[2,72,128]{2,1,0:T(8,128)S(1)}, u32[]{:S(2)}, u32[]{:S(2)}) collective-permute-start(f32[2,72,128]{2,1,0:T(8,128)S(1)} %pad_maximum_fusion.2), channel_id=1, source_target_pairs={{0,8},{1,9},{2,10},{3,11},{4,12},{5,13},{6,14},{7,15},{8,0},{9,1},... | collective-permute-start | bytes 221192 | tf_op jit(solution)/shard_map/ppermute | solution.py:341
  19.4 43.0 %all-to-all-start = ((f32[16,96,256]{2,1,0:T(8,128)}), f32[16,96,256]{2,1,0:T(8,128)S(1)}, u32[]{:S(2)}, u32[]{:S(2)}) async-start(f32[16,96,256]{2,1,0:T(8,128)} %turn.1), calls=%async_computation | async-start | bytes 3145728 | tf_op jit(solution)/shard_map/all_to_all | solution.py:403
  26.2 8.9 %collective-permute-start.4 = (f32[2,64,128]{2,1,0:T(8,128)S(1)}, f32[2,64,128]{2,1,0:T(8,128)S(1)}, u32[]{:S(2)}, u32[]{:S(2)}) collective-permute-start(f32[2,64,128]{2,1,0:T(8,128)S(1)} %fusion), channel_id=1, source_target_pairs={{0,2},{1,3},{2,0},{3,1},{4,6},{5,7},{6,4},{7,5},{8,10},{9,11},{10,... | collective-permute-start | bytes 196616 | tf_op jit(solution)/shard_map/ppermute | solution.py:341
  35.2 1.9 %collective-permute-start.5 = (f32[2,128,128]{2,1,0:T(8,128)S(1)}, f32[2,128,128]{2,1,0:T(8,128)S(1)}, u32[]{:S(2)}, u32[]{:S(2)}) collective-permute-start(f32[2,128,128]{2,1,0:T(8,128)S(1)} %pad_maximum_fusion.half_ref), channel_id=1, source_target_pairs={{0,1},{1,0},{2,3},{3,2},{4,5},{5,4},{6,7},{7,6},{8,9},{9,8},{10,11... | collective-permute-start | bytes 393224 | tf_op jit(solution)/shard_map/ppermute | solution.py:341

commit v5 on v4

--- a/solution.py
+++ b/solution.py
@@ -85,7 +85,7 @@
     return jnp.broadcast_to(row, (8, n)).T[:, 0:1]
 
 
-def sweep(work, r_ref, w_ref, b=32, bi=8):
+def sweep(work, r_ref, w_ref, b=32, bi=16):
     n = work.shape[0]
     groups = b // 8
     lane = lax.broadcasted_iota(jnp.int32, (8, n), 1)
@@ -123,7 +123,10 @@
                 for k2 in range(kk + 1, bi):
                     entry = jnp.broadcast_to(col[k2, own_group][s : s + 1, :], (8, 128))
                     for g in range(own_group, groups):
-                        col[k2, g] = col[k2, g] - mult[g] * entry
+                        if k2 == kk + 1:
+                            col[k2, g] = col[k2, g] - (col[kk, g] * entry) * inverse
+                        else:
+                            col[k2, g] = col[k2, g] - mult[g] * entry
                 pivot_row = jnp.broadcast_to(rows[own_group][s : s + 1, :], (8, n))
                 pivot_diag = jnp.broadcast_to(diag[own_group][s : s + 1, :], (8, 128))
                 for g in range(own_group, groups):
@@ -157,7 +160,7 @@
     return jnp.where(column < row, 0.0, matrix)
 
 
-def gram_kernel(row_scale, own_ref, x_ref, mask_ref, keep_ref, send_ref, a_ref, n1_ref, n2_ref, n3_ref, n4_ref):
+def gram_kernel(row_scale, own_ref, x_ref, mask_ref, mine_ref, core_ref, side_ref, both_ref, a_ref, n1_ref, n2_ref, n3_ref, n4_ref):
     rows, n = x_ref.shape
     peak = jnp.zeros((8, n), F32)
     for c in range(rows // 128):
@@ -173,7 +176,7 @@
             ref[at, :] = part
     pair = gram_pair(n1_ref[...], n2_ref[...], n3_ref[...], n4_ref[...])
     column, grow = column_of(top), top * row_scale
-    odd = (own_ref[0] & 1) > 0
+    refs = (mine_ref, core_ref, side_ref, both_ref)
     live = jnp.sum(mask_ref[...].astype(F32), axis=(0, 1), keepdims=True)
     lane = lax.broadcasted_iota(jnp.int32, (8, 128), 1)
     row = lax.broadcasted_iota(jnp.int32, (8, 128), 0)
@@ -185,24 +188,12 @@
         second = jnp.where(upper_half(), value[0:128, 0:128], last)
         extra = jnp.sum(jnp.where(diagonal(), last, 0.0), axis=0, keepdims=True)
         extra = jnp.where(row == 1, extra, count if index == 0 else 0.0)
-        size = first.shape[0]
-        keep_ref[index, 0:size] = jnp.where(odd, second, first)
-        send_ref[index, 0:size] = jnp.where(odd, first, second)
-        for ref in (keep_ref, send_ref):
+        size = first.shape[0] // 2
+        for turn, ref in enumerate(refs):
+            place = own_ref[0] ^ turn
+            block = jnp.where((place & 1) > 0, second, first)
+            ref[index, 0:size] = jnp.where((place & 2) > 0, block[size:], block[:size])
             ref[index, size:] = extra
-
-
-def quarter_kernel(own_ref, keep_ref, got_ref, mine_ref, send_ref):
-    size = mine_ref.shape[1] - 8
-    place = (own_ref[0] >> 1) & 1
-    for turn, ref in enumerate((mine_ref, send_ref)):
-        for to, at in (
-            (pl.ds(0, size), pl.ds(pl.multiple_of((place ^ turn) * size, 8), size)),
-            (pl.ds(size, 8), pl.ds(2 * size, 8)),
-        ):
-            ref[0, to, :], ref[1, to, :] = add_pair(
-                (keep_ref[0, at, :], keep_ref[1, at, :]), (got_ref[0, at, :], got_ref[1, at, :])
-            )
 
 
 def upper_half():
@@ -307,12 +298,18 @@
         rows_ref[pl.ds(at + 8, slots), :] = block[8:]
         return start + counts_ref[s]
 
-    lax.fori_loop(0, n, place, jnp.int32(0))
+    lax.fori_loop(0, n, place, jnp.int32(0), unroll=4)
     step = out_ref.shape[0] // sem.shape[0]
     copies = []
     for c in range(sem.shape[0]):
         at = pl.ds(c * step, step)
-        done_ref[at, :] = dot6(rows_ref[at, :], inv_ref[...], 1, 1)
+        done_ref[at, :] = lax.dot_general(
+            rows_ref[at, :],
+            inv_ref[...],
+            (((1,), (1,)), ((), ())),
+            precision=lax.Precision.HIGHEST,
+            preferred_element_type=F32,
+        )
         copies.append(pltpu.make_async_copy(done_ref.at[at], out_ref.at[at], sem.at[c]))
         copies[-1].start()
     for copy in copies:
@@ -354,22 +351,19 @@
     mask = fluid_mask.reshape(cells // 128, 128)
     block = jnp.arange(cells // 128)
     starts = jnp.sum(jnp.where(block[None, :, None] < block[:, None, None], mask[None], 0), (1, 2))
-    half = jax.ShapeDtypeStruct((2, 136, 128), F32)
-    keep, send = call(
+    size = 64
+    quarter = jax.ShapeDtypeStruct((2, size + 8, 128), F32)
+    mine, *sent = call(
         functools.partial(gram_kernel, 1.0 / (n * BLK)),
         "gram",
-        [half, half],
+        [quarter] * 4,
         [SMEM, VMEM, VMEM],
         [pltpu.VMEM((cells, k), F32)] + [pltpu.VMEM((cells, k), jnp.bfloat16)] * 4,
         16 * cells * k * k,
         (own_list, snapshots, mask),
     )
-    size = (keep.shape[1] - 8) // 2
-    quarter = jax.ShapeDtypeStruct((2, size + 8, 128), F32)
-    mine, sent = call(
-        quarter_kernel, "quarter", [quarter] * 2, [SMEM, VMEM, VMEM], [], 1 << 20, (own_list, keep, other(send, 1, n))
-    )
-    got = other(sent, 2, n)
+    got = [other(x, turn, n) for turn, x in zip((3, 2, 1), sent[::-1])]
+    mine = add(add(mine, got[2]), add(got[1], got[0]))
     starts, mine = lax.optimization_barrier((starts, mine))
     blocks = call(
         functools.partial(compact_kernel, n),
@@ -380,12 +374,13 @@
         4 << 30,
         (starts, mask, snapshots),
     )
-    got, blocks = lax.optimization_barrier((got, blocks))
-    mine = add(mine, got)
     bit = 4
     while bit < n:
         near_counts = mine[0, size, :n].astype(jnp.int32)
-        mine = add(mine, other(mine, bit, n))
+        got = other(mine, bit, n)
+        if bit == 4:
+            got, blocks = lax.optimization_barrier((got, blocks))
+        mine = add(mine, got)
         bit *= 2
     counts = mine[0, size, :n].astype(jnp.int32)
     extra = mine[:, size:]

time: 65.8 us -> 65.8 us (level)
  waiting for transfers between devices: 19.7 us -> 23 us
  Pallas kernels: 30.3 us -> 27.3 us
    pallas_call x6 -> x5, Pallas kernels: 30.3 us -> 27.3 us  [call(): pl.pallas_call(kernel, name=name, out_shape=out, in_specs=in_specs, out_s...]
    all_to_all x1, waiting for transfers between devices: 6.34 us -> 9.28 us  [local(): lax.all_to_all(outgoing, 'height', split_axis=0, concat_axis=0, tiled=True)]
    all_to_all x1, starting transfers between devices: 6.8 us -> 5.19 us  [local(): lax.all_to_all(outgoing, 'height', split_axis=0, concat_axis=0, tiled=True)]
    ppermute x6 -> x7, starting transfers between devices: 4.93 us -> 6.34 us  [other(): return lax.ppermute(x, 'height', [(i, i ^ bits) for i in range(n)])]
    ppermute x6 -> x7, waiting for transfers between devices: 13.4 us -> 13.7 us  [other(): return lax.ppermute(x, 'height', [(i, i ^ bits) for i in range(n)])]
  transfers between devices with their start and end apart: 7 -> 8, of which waited for: 6 -> 6; matrix products, arithmetic and copies ran while one was open for 1% -> 1% of each run, Pallas kernels for 36% -> 32%
where the time goes in v5:
time: 65.8 us; the launch traced here: 65.5 us
  Pallas kernels  27.3 us (41%)
  waiting for transfers between devices  23 us (35%)
  starting transfers between devices  11.5 us (17%)
  local copies, waits for them, and re-layouts  2.29 us (3%)
  between operations  0.89 us (1%)
    pallas_call x5, Pallas kernels, call(): pl.pallas_call(kernel, name=name, out_shape=out, in_specs=in_specs, out_s...  27.3 us
    ppermute x7, waiting for transfers between devices, other(): return lax.ppermute(x, 'height', [(i, i ^ bits) for i in range(n)])  13.7 us
    all_to_all x1, waiting for transfers between devices, local(): lax.all_to_all(outgoing, 'height', split_axis=0, concat_axis=0, tiled=True)  9.28 us
    ppermute x7, starting transfers between devices, other(): return lax.ppermute(x, 'height', [(i, i ^ bits) for i in range(n)])  6.34 us
    all_to_all x1, starting transfers between devices, local(): lax.all_to_all(outgoing, 'height', split_axis=0, concat_axis=0, tiled=True)  5.19 us
    unnamed x8, local copies, waits for them, and re-layouts  2.29 us
  transfers between devices with their start and end apart: 8, of which 6 were waited for; matrix products, arithmetic and copies ran while one was open for 1% of the time, Pallas kernels for 32%

profile of v5, /device:TPU:13, one launch (start us, length us, event | category | flops | bytes accessed | tf_op | source)
XLA Modules:
  0.0 65.5 jit_solution(11807916633772715831)
XLA Ops:
  0.6 0.0 copy-start
  0.6 0.7 %copy-done = s32[2048]{0:T(1024)S(1)} copy-done((s32[2048]{0:T(1024)S(1)}, s32[2048]{0:T(1024)}, u32[]{:S(2)}) %copy-start) | copy-done | bytes 8216
  1.3 0.0 copy-start.2
  1.3 1.6 %copy-done.2 = f32[2048,256]{1,0:T(8,128)S(1)} copy-done((f32[2048,256]{1,0:T(8,128)S(1)}, f32[2048,256]{1,0:T(8,128)}, u32[]{:S(2)}) %copy-start.2) | copy-done | bytes 2097176
  2.9 0.0 copy-start.1
  2.9 0.0 copy-start.3
  2.9 3.8 %gram.1 = (f32[2,72,128]{2,1,0:T(8,128)S(1)}, f32[2,72,128]{2,1,0:T(8,128)S(1)}, f32[2,72,128]{2,1,0:T(8,128)S(1)}, f32[2,72,128]{2,1,0:T(8,128)S(1)}) custom-call(s32[1]{0:T(128)} %bitcast.own_ref, f32[2048,256]{1,0:T(8,128)S(1)} %copy-done.2, s32[16,128]{1,0:T(8,128)S(1)} %bitcast.6), custom_call_target="tpu_custom_call" | custom-call | flops 2147483648 | bytes 4194304 | tf_op jit(solution)/shard_map/gram/pallas_call | solution.py:325
  6.7 0.7 %collective-permute-start = (f32[2,72,128]{2,1,0:T(8,128)S(1)}, f32[2,72,128]{2,1,0:T(8,128)S(1)}, u32[]{:S(2)}, u32[]{:S(2)}) collective-permute-start(f32[2,72,128]{2,1,0:T(8,128)S(1)} %get-tuple-element.13), channel_id=1, source_target_pairs={{0,1},{1,0},{2,3},{3,2},{4,5},{5,4},{6,7},{7,6},{8,9},{9,8},{10,11... | collective-permute-start | bytes 221192 | tf_op jit(solution)/shard_map/ppermute | solution.py:338
  7.4 0.2 collective-permute-start.1
  7.7 1.5 %collective-permute-start.2 = (f32[2,72,128]{2,1,0:T(8,128)S(1)}, f32[2,72,128]{2,1,0:T(8,128)S(1)}, u32[]{:S(2)}, u32[]{:S(2)}) collective-permute-start(f32[2,72,128]{2,1,0:T(8,128)S(1)} %get-tuple-element.15), channel_id=1, source_target_pairs={{0,3},{1,2},{2,1},{3,0},{4,7},{5,6},{6,5},{7,4},{8,11},{9,10},{10,... | collective-permute-start | bytes 221192 | tf_op jit(solution)/shard_map/ppermute | solution.py:338
  9.2 0.5 select_reduce_fusion.starts_ref
  9.6 0.0 collective-permute-done
  9.6 1.7 %collective-permute-done.1 = f32[2,72,128]{2,1,0:T(8,128)S(1)} collective-permute-done((f32[2,72,128]{2,1,0:T(8,128)S(1)}, f32[2,72,128]{2,1,0:T(8,128)S(1)}, u32[]{:S(2)}, u32[]{:S(2)}) %collective-permute-start.1) | collective-permute-done | bytes 73760 | tf_op jit(solution)/shard_map/ppermute | solution.py:338
  11.3 1.7 %collective-permute-done.2 = f32[2,72,128]{2,1,0:T(8,128)S(1)} collective-permute-done((f32[2,72,128]{2,1,0:T(8,128)S(1)}, f32[2,72,128]{2,1,0:T(8,128)S(1)}, u32[]{:S(2)}, u32[]{:S(2)}) %collective-permute-start.2) | collective-permute-done | bytes 73760 | tf_op jit(solution)/shard_map/ppermute | solution.py:338
  13.1 0.2 collective-permute-start.3
  13.3 0.0 copy-done.1
  13.3 0.0 copy-done.3
  13.3 2.7 %compact.1.blocks_ref = f32[16,96,256]{2,1,0:T(8,128)S(1)} custom-call(s32[16]{0:T(128)S(1)} %select_reduce_fusion.starts_ref, s32[16,128]{1,0:T(8,128)S(1)} %bitcast.8, f32[2048,256]{1,0:T(8,128)S(1)} %copy-done.3), custom_call_target="tpu_custom_call" | custom-call | flops 4294967296 | bytes 4194304 | tf_op jit(solution)/shard_map/compact/pallas_call | solution.py:325
  16.1 0.7 %collective-permute-done.3 = f32[2,72,128]{2,1,0:T(8,128)S(1)} collective-permute-done((f32[2,72,128]{2,1,0:T(8,128)S(1)}, f32[2,72,128]{2,1,0:T(8,128)S(1)}, u32[]{:S(2)}, u32[]{:S(2)}) %collective-permute-start.3) | collective-permute-done | bytes 73760 | tf_op jit(solution)/shard_map/ppermute | solution.py:338
  16.8 2.4 %collective-permute-start.4 = (f32[2,72,128]{2,1,0:T(8,128)S(1)}, f32[2,72,128]{2,1,0:T(8,128)S(1)}, u32[]{:S(2)}, u32[]{:S(2)}) collective-permute-start(f32[2,72,128]{2,1,0:T(8,128)S(1)} %pad_maximum_fusion.2), channel_id=1, source_target_pairs={{0,8},{1,9},{2,10},{3,11},{4,12},{5,13},{6,14},{7,15},{8,0},{9,1},... | collective-permute-start | bytes 221192 | tf_op jit(solution)/shard_map/ppermute | solution.py:338
  19.2 1.9 %turn.1 = f32[16,96,256]{2,1,0:T(8,128)} custom-call(s32[1]{0:T(128)} %bitcast.own_ref, s32[16]{0:T(128)S(1)} %fusion.7.counts_ref, f32[16,96,256]{2,1,0:T(8,128)S(1)} %compact.1.blocks_ref), custom_call_target="tpu_custom_call" | custom-call | flops 1048576 | bytes 4194304 | tf_op jit(solution)/shard_map/turn/pallas_call | solution.py:325
  21.1 5.2 %all-to-all-start = ((f32[16,96,256]{2,1,0:T(8,128)}), f32[16,96,256]{2,1,0:T(8,128)S(1)}, u32[]{:S(2)}, u32[]{:S(2)}) async-start(f32[16,96,256]{2,1,0:T(8,128)} %turn.1), calls=%async_computation | async-start | bytes 3145728 | tf_op jit(solution)/shard_map/all_to_all | solution.py:398
  26.3 0.0 collective-permute-done.4
  26.3 0.3 collective-permute-start.5
  26.7 8.6 %collective-permute-done.5 = f32[2,64,128]{2,1,0:T(8,128)S(1)} collective-permute-done((f32[2,64,128]{2,1,0:T(8,128)S(1)}, f32[2,64,128]{2,1,0:T(8,128)S(1)}, u32[]{:S(2)}, u32[]{:S(2)}) %collective-permute-start.5) | collective-permute-done | bytes 65568 | tf_op jit(solution)/shard_map/ppermute | solution.py:338
  35.3 0.9 %collective-permute-start.6 = (f32[2,128,128]{2,1,0:T(8,128)S(1)}, f32[2,128,128]{2,1,0:T(8,128)S(1)}, u32[]{:S(2)}, u32[]{:S(2)}) collective-permute-start(f32[2,128,128]{2,1,0:T(8,128)S(1)} %pad_maximum_fusion.half_ref), channel_id=1, source_target_pairs={{0,1},{1,0},{2,3},{3,2},{4,5},{5,4},{6,7},{7,6},{8,9},{9,8},{10,11... | collective-permute-start | bytes 393224 | tf_op jit(solution)/shard_map/ppermute | solution.py:338
  36.3 1.0 %collective-permute-done.6.got_ref = f32[2,128,128]{2,1,0:T(8,128)S(1)} collective-permute-done((f32[2,128,128]{2,1,0:T(8,128)S(1)}, f32[2,128,128]{2,1,0:T(8,128)S(1)}, u32[]{:S(2)}, u32[]{:S(2)}) %collective-permute-start.6) | collective-permute-done | bytes 131104 | tf_op jit(solution)/shard_map/ppermute | solution.py:338
  37.2 16.0 %chain.1 = (f32[256,256]{1,0:T(8,128)S(1)}, f32[256,256]{1,0:T(8,128)}) custom-call(s32[1]{0:T(128)} %bitcast.own_ref, f32[2,128,128]{2,1,0:T(8,128)S(1)} %pad_maximum_fusion.half_ref, f32[2,128,128]{2,1,0:T(8,128)S(1)} %collective-permute-done.6.got_ref, f32[2,8,128]{2,1,0:T(8,128)S(1)} %pad_maximum_fusion.3.extra_ref), custom_call_target="tpu_custom_call" | custom-call | flops 21474836480 | bytes 4194304 | tf_op jit(solution)/shard_map/chain/pallas_call | solution.py:325
  53.2 9.3 %all-to-all-done.recv_ref = f32[16,96,256]{2,1,0:T(8,128)S(1)} async-done(((f32[16,96,256]{2,1,0:T(8,128)}), f32[16,96,256]{2,1,0:T(8,128)S(1)}, u32[]{:S(2)}, u32[]{:S(2)}) %all-to-all-start) | async-done | bytes 1572896 | tf_op jit(solution)/shard_map/all_to_all | solution.py:398
  62.5 2.8 %modes.1 = f32[1024,256]{1,0:T(8,128)} custom-call(s32[1]{0:T(128)} %bitcast.own_ref, s32[16]{0:T(128)S(1)} %fusion.8.counts_ref, f32[16,96,256]{2,1,0:T(8,128)S(1)} %all-to-all-done.recv_ref, f32[256,256]{1,0:T(8,128)S(1)} %get-tuple-element.20.inv_ref), custom_call_target="tpu_custom_call" | custom-call | flops 805306368 | bytes 4194304 | tf_op jit(solution)/shard_map/modes/pallas_call | solution.py:325
  (12 shorter events, 0.1 us)
Async XLA Ops:
  0.6 0.7 %copy-start = (s32[2048]{0:T(1024)S(1)}, s32[2048]{0:T(1024)}, u32[]{:S(2)}) copy-start(s32[2048]{0:T(1024)} %param.3) | copy-start | bytes 24580
  1.3 1.6 %copy-start.2 = (f32[2048,256]{1,0:T(8,128)S(1)}, f32[2048,256]{1,0:T(8,128)}, u32[]{:S(2)}) copy-start(f32[2048,256]{1,0:T(8,128)} %x_ref.3) | copy-start | bytes 6291460
  2.9 10.4 %copy-start.1 = (s32[2048]{0:T(1024)S(1)}, s32[2048]{0:T(1024)}, u32[]{:S(2)}) copy-start(s32[2048]{0:T(1024)} %param.3) | copy-start | bytes 24580
  2.9 10.4 %copy-start.3 = (f32[2048,256]{1,0:T(8,128)S(1)}, f32[2048,256]{1,0:T(8,128)}, u32[]{:S(2)}) copy-start(f32[2048,256]{1,0:T(8,128)} %x_ref.3) | copy-start | bytes 6291460
  6.7 2.9 %collective-permute-start = (f32[2,72,128]{2,1,0:T(8,128)S(1)}, f32[2,72,128]{2,1,0:T(8,128)S(1)}, u32[]{:S(2)}, u32[]{:S(2)}) collective-permute-start(f32[2,72,128]{2,1,0:T(8,128)S(1)} %get-tuple-element.13), channel_id=1, source_target_pairs={{0,1},{1,0},{2,3},{3,2},{4,5},{5,4},{6,7},{7,6},{8,9},{9,8},{10,11... | collective-permute-start | bytes 221192 | tf_op jit(solution)/shard_map/ppermute | solution.py:338
  7.4 3.8 %collective-permute-start.1 = (f32[2,72,128]{2,1,0:T(8,128)S(1)}, f32[2,72,128]{2,1,0:T(8,128)S(1)}, u32[]{:S(2)}, u32[]{:S(2)}) collective-permute-start(f32[2,72,128]{2,1,0:T(8,128)S(1)} %get-tuple-element.14), channel_id=1, source_target_pairs={{0,2},{1,3},{2,0},{3,1},{4,6},{5,7},{6,4},{7,5},{8,10},{9,11},{10,... | collective-permute-start | bytes 221192 | tf_op jit(solution)/shard_map/ppermute | solution.py:338
  7.7 5.3 %collective-permute-start.2 = (f32[2,72,128]{2,1,0:T(8,128)S(1)}, f32[2,72,128]{2,1,0:T(8,128)S(1)}, u32[]{:S(2)}, u32[]{:S(2)}) collective-permute-start(f32[2,72,128]{2,1,0:T(8,128)S(1)} %get-tuple-element.15), channel_id=1, source_target_pairs={{0,3},{1,2},{2,1},{3,0},{4,7},{5,6},{6,5},{7,4},{8,11},{9,10},{10,... | collective-permute-start | bytes 221192 | tf_op jit(solution)/shard_map/ppermute | solution.py:338
  13.1 3.7 %collective-permute-start.3 = (f32[2,72,128]{2,1,0:T(8,128)S(1)}, f32[2,72,128]{2,1,0:T(8,128)S(1)}, u32[]{:S(2)}, u32[]{:S(2)}) collective-permute-start(f32[2,72,128]{2,1,0:T(8,128)S(1)} %pad_maximum_fusion.1), channel_id=1, source_target_pairs={{0,4},{1,5},{2,6},{3,7},{4,0},{5,1},{6,2},{7,3},{8,12},{9,13},{10,... | collective-permute-start | bytes 221192 | tf_op jit(solution)/shard_map/ppermute | solution.py:338
  16.8 9.5 %collective-permute-start.4 = (f32[2,72,128]{2,1,0:T(8,128)S(1)}, f32[2,72,128]{2,1,0:T(8,128)S(1)}, u32[]{:S(2)}, u32[]{:S(2)}) collective-permute-start(f32[2,72,128]{2,1,0:T(8,128)S(1)} %pad_maximum_fusion.2), channel_id=1, source_target_pairs={{0,8},{1,9},{2,10},{3,11},{4,12},{5,13},{6,14},{7,15},{8,0},{9,1},... | collective-permute-start | bytes 221192 | tf_op jit(solution)/shard_map/ppermute | solution.py:338
  21.1 41.4 %all-to-all-start = ((f32[16,96,256]{2,1,0:T(8,128)}), f32[16,96,256]{2,1,0:T(8,128)S(1)}, u32[]{:S(2)}, u32[]{:S(2)}) async-start(f32[16,96,256]{2,1,0:T(8,128)} %turn.1), calls=%async_computation | async-start | bytes 3145728 | tf_op jit(solution)/shard_map/all_to_all | solution.py:398
  26.3 8.9 %collective-permute-start.5 = (f32[2,64,128]{2,1,0:T(8,128)S(1)}, f32[2,64,128]{2,1,0:T(8,128)S(1)}, u32[]{:S(2)}, u32[]{:S(2)}) collective-permute-start(f32[2,64,128]{2,1,0:T(8,128)S(1)} %fusion), channel_id=1, source_target_pairs={{0,2},{1,3},{2,0},{3,1},{4,6},{5,7},{6,4},{7,5},{8,10},{9,11},{10,... | collective-permute-start | bytes 196616 | tf_op jit(solution)/shard_map/ppermute | solution.py:338
  35.3 1.9 %collective-permute-start.6 = (f32[2,128,128]{2,1,0:T(8,128)S(1)}, f32[2,128,128]{2,1,0:T(8,128)S(1)}, u32[]{:S(2)}, u32[]{:S(2)}) collective-permute-start(f32[2,128,128]{2,1,0:T(8,128)S(1)} %pad_maximum_fusion.half_ref), channel_id=1, source_target_pairs={{0,1},{1,0},{2,3},{3,2},{4,5},{5,4},{6,7},{7,6},{8,9},{9,8},{10,11... | collective-permute-start | bytes 393224 | tf_op jit(solution)/shard_map/ppermute | solution.py:338
